TPU v7x, 256 devices: a whole 4x4x8 slice. The times are simulated.
256 devices in a mesh: step: 32 (over z, x), seq: 8 (over y, core).
Axes of the slice: x: 4, y: 4, z: 8, core: 2. Of those that a mesh axis runs over, the one named last changes fastest.
Arguments:
- latents: bfloat16 [32, 8, 256, 1152], P('step', 'seq'), may hold values from -6 to 6
- timesteps: int32 [32], P('step'), may hold values from 0 to 31
- step_sizes: float32 [32], P('step'), may hold values from 0.02 to 0.15
- modulation: bfloat16 [32, 6912], replicated, may hold values from -4 to 4
- spatial_qkv: bfloat16 [1152, 1728], replicated, may hold values from -0.1875 to 0.1875
- spatial_out: bfloat16 [576, 1152], replicated, may hold values from -0.25 to 0.25
- temporal_qkv: bfloat16 [1152, 1728], replicated, may hold values from -0.1875 to 0.1875
- temporal_out: bfloat16 [576, 1152], replicated, may hold values from -0.25 to 0.25
Outputs:
- updated: bfloat16 [32, 8, 256, 1152], P('step', 'seq')
- change: float32 [32], P('step')
All inputs are finite; a program needn't handle non-finite values.
Results may differ from a plain program's by a relative error of at most 0.01.
Values may be sent and summed in bfloat16 or wider, within the bound.
A program may use at most 128 MiB of HBM per device.

v0:
```python
import math

import jax
import jax.numpy as jnp
from jax import lax
from jax.sharding import PartitionSpec as P

HEADS = 8
HEAD_DIM = 72


def shifted(block, axis, distance):
    devices = range(lax.axis_size(axis))
    route = [(i - distance, i) for i in devices if i - distance in devices]
    return lax.ppermute(block, axis, route)


def spread_2(value, axis, source):
    kept = jnp.where(lax.axis_index(axis) == source, value, 0).astype(value.dtype)
    return lax.psum(kept, axis)


def entering(x, axis, combine, identity):
    size, place = (lax.axis_size(axis), lax.axis_index(axis))
    everything = lax.all_gather(x.astype(jnp.bfloat16), axis)
    start = jnp.broadcast_to(jnp.asarray(identity, x.dtype), x.shape)

    def turn(k, before):
        reached = k < place
        new = combine(before, everything[k].astype(x.dtype))
        return jnp.where(reached, new, before)

    return lax.fori_loop(0, size, turn, start)


def layer_norm(values):
    values = values.astype(jnp.float32)
    center = values - jnp.mean(values, axis=-1, keepdims=True)
    spread = jnp.mean(center * center, axis=-1, keepdims=True)
    return center * lax.rsqrt(spread + 1e-06)


def unit_rows(values):
    return values * lax.rsqrt(jnp.mean(values * values, axis=-1, keepdims=True) + 1e-06)


def attend(inputs, w_project):
    batch, length = (inputs.shape[0], inputs.shape[1])
    projected = jnp.einsum("bld,de->ble", inputs, w_project, preferred_element_type=jnp.float32)
    projected = projected.reshape(batch, length, 3, HEADS, HEAD_DIM)
    queries = unit_rows(projected[:, :, 0]).astype(jnp.bfloat16)
    keys = unit_rows(projected[:, :, 1]).astype(jnp.bfloat16)
    values = projected[:, :, 2].astype(jnp.bfloat16)
    scores = jnp.einsum("blhe,bmhe->bhlm", queries, keys, preferred_element_type=jnp.float32)
    scores = scores * (3.0 / math.sqrt(HEAD_DIM))
    exponent = jnp.exp(scores)
    weights = (exponent / jnp.sum(exponent, axis=-1, keepdims=True)).astype(jnp.bfloat16)
    mixed = jnp.einsum("bhlm,bmhe->blhe", weights, values, preferred_element_type=jnp.float32)
    return mixed.astype(jnp.bfloat16).reshape(batch, length, HEADS * HEAD_DIM)


def project_out(heads_out, w_out):
    return jnp.einsum("ble,ed->bld", heads_out, w_out, preferred_element_type=jnp.float32)


def body(
    latents, timesteps, step_sizes, modulation, spatial_qkv, spatial_out, temporal_qkv, temporal_out
):
    state = latents[0]
    width = state.shape[-1]
    table_rows = modulation.shape[0]
    one_hot = (jnp.arange(table_rows, dtype=jnp.int32) == timesteps[0]).astype(jnp.bfloat16)[
        None, :
    ]
    conditioning = jnp.dot(one_hot, modulation, preferred_element_type=jnp.float32).reshape(
        6, width
    )
    step_size = step_sizes[0]
    following = shifted(latents, "step", -1)
    spatial_in = (layer_norm(state) * (1.0 + conditioning[1]) + conditioning[0]).astype(
        jnp.bfloat16
    )
    spatial_heads = attend(spatial_in, spatial_qkv)
    after_spatial = (
        state.astype(jnp.float32) + conditioning[2] * project_out(spatial_heads, spatial_out)
    ).astype(jnp.bfloat16)
    temporal_in = (layer_norm(after_spatial) * (1.0 + conditioning[4]) + conditioning[3]).astype(
        jnp.bfloat16
    )
    gathered = jnp.swapaxes(
        attend(
            jnp.swapaxes(
                lax.all_to_all(temporal_in, "seq", split_axis=1, concat_axis=0, tiled=True), 0, 1
            ),
            temporal_qkv,
        ),
        0,
        1,
    )
    temporal_heads = lax.all_to_all(gathered, "seq", split_axis=0, concat_axis=1, tiled=True)
    drift_term = step_size * (
        after_spatial.astype(jnp.float32)
        + conditioning[5] * project_out(temporal_heads, temporal_out)
    )
    anchor_part = spread_2(state, "step", 0).astype(jnp.float32)
    earlier_sum = entering(
        drift_term, "step", lambda earlier, later: earlier + later, jnp.zeros_like(drift_term)
    )
    running = earlier_sum + drift_term
    updated = (anchor_part + running).astype(jnp.bfloat16)
    difference = updated.astype(jnp.float32) - following[0].astype(jnp.float32)
    local_sum = jnp.sum(difference * difference)
    total = lax.psum(local_sum, "seq")
    entries = lax.axis_size("seq") * state.shape[0] * state.shape[1] * state.shape[2]
    change = (total / entries).reshape(1)
    return (updated[None], change)


def solution(mesh):
    in_specs = (P("step", "seq", None, None), P("step"), P("step"), P(), P(), P(), P(), P())
    out_specs = (P("step", "seq", None, None), P("step"))
    return jax.shard_map(body, mesh=mesh, in_specs=in_specs, out_specs=out_specs, check_vma=False)
```

profile of v0, /device:TPU:33, one launch (start us, length us, event | category | flops | bytes accessed | tf_op | source)
XLA Modules:
  0.0 409.4 jit_solution(15964048497142923567)
XLA Ops:
  10.7 3.7 convolution_bitcast_fusion
  17.8 1.9 copy.73
  20.2 6.0 %reduce.15 = bf16[256,1152]{1,0:T(8,128)(2,1)} reduce(bf16[256,1,1152]{2,1,0:T(2,128)(2,1)} %bitcast.118, bf16[]{:T(256)} %broadcast.240), dimensions={1}, to_apply=%bitcast.113.reduce_sub_computation | reduce | bytes 1179650
  26.2 2.5 reshape.411
  28.8 15.6 %all_to_all.21 = bf16[8,2,18432]{2,1,0:T(2,128)(2,1)} all-to-all(bf16[8,2,18432]{2,1,0:T(2,128)(2,1)} %reshape.411), channel_id=1, replica_groups=mesh['step'=32,'seq'=8] {'seq'}, dimensions={0} | all-to-all | bytes 1179648 | tf_op jit(solution)/shard_map/all_to_all | solution.py:93
  44.4 3.5 reshape.412
  49.2 4.8 %fusion = f32[32,8,1728]{2,1,0:T(8,128)} fusion(bf16[1152,1728]{0,1:T(8,128)(2,1)} %param.16, bf16[8,32,1152]{2,1,0:T(8,128)(2,1)S(1)} %bitcast.123), kind=kOutput, calls=%fused_computation.1 | convolution fusion | flops 1019215872 | bytes 6340608 | tf_op jit(solution)/shard_map/bld,de->ble/dot_general | solution.py:49
  54.1 4.0 reshape.397
  58.1 1.7 fusion.52
  59.8 2.1 slice.65
  62.7 1.8 fusion.8
  64.4 3.1 fusion.9
  67.6 1.9 copy.42
  71.7 4.1 all-to-all-start.1
  76.5 6.5 %all-to-all-done.1 = bf16[8,32,576]{2,1,0:T(8,128)(2,1)S(1)} async-done(((bf16[8,32,576]{2,1,0:T(8,128)(2,1)}), bf16[8,32,576]{2,1,0:T(8,128)(2,1)S(1)}, u32[]{:S(2)}, u32[]{:S(2)}) %all-to-all-start.1) | async-done | bytes 294944 | tf_op jit(solution)/shard_map/all_to_all | solution.py:100
  83.0 1.9 fusion.55
  84.9 3.9 collective-permute-start
  89.7 145.6 %all-gather.3.cloned.1.call-done = bf16[8192,1152]{1,0:T(8,128)(2,1)} async-done(((bf16[256,1152]{1,0:T(8,128)(2,1)}), bf16[8192,1152]{1,0:T(8,128)(2,1)}) %all-gather.3.cloned.1.call-update) | async-done | bytes 18874384 | tf_op jit(solution)/shard_map/all_gather | solution.py:25
  235.3 54.3 %while.14 = (s32[]{:T(128)}, f32[1,256,1152]{2,1,0:T(8,128)S(1)}, s32[]{:T(128)}, bf16[32,1,256,1152]{3,2,1,0:T(8,128)(2,1)}, s32[]{:T(128)}, /*index=5*/s32[]{:T(128)}) while((s32[]{:T(128)}, f32[1,256,1152]{2,1,0:T(8,128)S(1)}, s32[]{:T(128)}, bf16[32,1,256,1152]{3,2,1,0:T(8,128)(2,1)}, s32[]{:T(128)}, ...), condition=%wide.region_12.13_spmd.clone, body=%wide.region_11.12_spmd.clone.sunk | while | flops 1179652 | bytes 2949213 | solution.py:33
  252.3 1.7 add_select_fusion.2
  267.6 1.7 add_select_fusion.2
  289.7 90.5 %all-reduce.2.cloned.1.call-done = bf16[1,256,1152]{2,1,0:T(8,128)(2,1)} async-done(((bf16[1,256,1152]{2,1,0:T(8,128)(2,1)}), bf16[1,256,1152]{2,1,0:T(8,128)(2,1)}) %all-reduce.2.cloned.1.call-update) | async-done | bytes 589840 | tf_op jit(solution)/shard_map/psum | solution.py:20
  380.2 3.3 fusion.18
  383.4 17.3 %psum.15 = f32[]{:T(128)} all-reduce(f32[]{:T(128)} %get-tuple-element.123), channel_id=1, replica_groups=mesh['step'=32,'seq'=8] {'seq'}, use_global_device_ids=true, to_apply=%region_14.15 | all-reduce | flops 1 | bytes 8 | tf_op jit(solution)/shard_map/psum | solution.py:113
  (66 shorter events, 62.2 us)
Async XLA Ops:
  7.2 75.8 %copy-start = (bf16[576,1152]{1,0:T(8,128)(2,1)S(1)}, bf16[576,1152]{1,0:T(8,128)(2,1)}, u32[]{:S(2)}) copy-start(bf16[576,1152]{1,0:T(8,128)(2,1)} %param.17) | copy-start | bytes 3981316
  7.2 3.2 copy-start.1
  15.1 1.3 copy-start.2
  71.7 11.2 %all-to-all-start.1 = ((bf16[8,32,576]{2,1,0:T(8,128)(2,1)}), bf16[8,32,576]{2,1,0:T(8,128)(2,1)S(1)}, u32[]{:S(2)}, u32[]{:S(2)}) async-start(bf16[8,32,576]{2,1,0:T(8,128)(2,1)} %copy.43), calls=%async_computation.1 | async-start | bytes 655360 | tf_op jit(solution)/shard_map/all_to_all | solution.py:100
  75.8 159.5 %all-gather.3.cloned.1.call-start = ((), (), s32[]{:S(2)}) async-start(), calls=%async_computation.3 | async-start | bytes 19464192 | tf_op jit(solution)/shard_map/all_gather | solution.py:25
  84.8 295.3 %all-reduce.2.cloned.1.call-start = ((), (), s32[]{:S(2)}) async-start(), calls=%async_computation.2 | async-start | bytes 1179648 | tf_op jit(solution)/shard_map/psum | solution.py:20
  84.9 295.3 %collective-permute-start = (bf16[1,1,256,1152]{3,2,1,0:T(8,128)(2,1)S(1)}, bf16[1,1,256,1152]{3,2,1,0:T(8,128)(2,1)}, u32[]{:S(2)}, u32[]{:S(2)}) collective-permute-start(bf16[1,1,256,1152]{3,2,1,0:T(8,128)(2,1)S(1)} %copy-done.1), channel_id=1, source_target_pairs={{8,0},{16,8},{24,16},{32,24},{40,32},{48,40},{56,48},{64,56},{72,6... | collective-permute-start | bytes 1769480 | tf_op jit(solution)/shard_map/ppermute | solution.py:15
Sparse Core Ops, SparseCore 0:
  85.0 150.3 all-gather.2
  238.7 141.4 all-reduce.1
where the time goes:
time: 414 us; the launch traced here: 409 us
  waiting for transfers between devices  243 us (59%)
  other arithmetic  66.7 us (16%)
  blocking collectives  32.9 us (8%)
  local copies, waits for them, and re-layouts  22.7 us (5%)
  matrix products  18.3 us (4%)
  between operations  17.4 us (4%)
  starting transfers between devices  8.06 us (2%)
    all_gather x1, waiting for transfers between devices, entering(): everything = lax.all_gather(x.astype(jnp.bfloat16), axis)  146 us
    psum x1, waiting for transfers between devices, spread_2(): return lax.psum(kept, axis)  90.5 us
    select_n x32, other arithmetic, turn(): return jnp.where(reached, new, before)  53.6 us
    psum x1, blocking collectives, body(): total = lax.psum(local_sum, 'seq')  17.3 us
    all_to_all x1, blocking collectives, body(): lax.all_to_all(temporal_in, 'seq', split_axis=1, concat_axis=0, tiled=True)  15.6 us
    unnamed x10, local copies, waits for them, and re-layouts  8.74 us
    dot_general x2, matrix products, attend(): jnp.einsum('bld,de->ble', inputs, w_project, preferred_element_type=jnp.f...  8.49 us
  transfers between devices with their start and end apart: 4, of which 3 were waited for; matrix products, arithmetic and copies ran while one was open for 13% of the time, Pallas kernels for 0%

commit v1 on v0

v1 whole, which is shorter than its diff:
```python
import math

import jax
import jax.numpy as jnp
from jax import lax
from jax.experimental import pallas as pl
from jax.experimental.pallas import tpu as pltpu
from jax.sharding import PartitionSpec as P

MESH = pl.DeviceIdType.MESH
F32 = jnp.float32
BF16 = jnp.bfloat16

D = 1152
HEADS = 8
HEAD_DIM = 72
E = HEADS * HEAD_DIM
ROWS = 256
HALF = 128
PIECE = 16
NX = 4
NZ = 8
NS = 8
WIDE = 640
SHIFT = 512
EPS = 1e-6
LOG2E = 1.4426950408889634
Q_SCALE = 3.0 / math.sqrt(HEAD_DIM) * LOG2E


def layer_norm(values):
    center = values - jnp.mean(values, axis=-1, keepdims=True)
    spread = jnp.mean(center * center, axis=-1, keepdims=True)
    return center * lax.rsqrt(spread + EPS)


def project(inputs, w_ref, member, spread, qk, vals):
    raw = jnp.dot(inputs, w_ref[:, : 2 * E], preferred_element_type=F32)
    squares = jnp.dot((raw * raw).astype(BF16), member[...], preferred_element_type=F32)
    group = lax.broadcasted_iota(jnp.int32, squares.shape, 1)
    root = lax.rsqrt(squares * (1.0 / HEAD_DIM) + EPS)
    root = root * jnp.where(group < HEADS, Q_SCALE, 1.0)
    high = root.astype(BF16)
    low = (root - high.astype(F32)).astype(BF16)
    factor = jnp.dot(
        jnp.concatenate([high, low], axis=1), spread[...], preferred_element_type=F32
    )
    units = (raw * factor).astype(BF16)
    qk[0, :, :E] = units[:, :E]
    qk[1, :, :E] = units[:, E:]
    vals[:, :E] = jnp.dot(inputs, w_ref[:, 2 * E :], preferred_element_type=F32).astype(BF16)


def attend(qk, vals, rows, mask):
    count = rows.size
    ones = jnp.ones((count, 128), BF16)
    tiles = [None] * 5
    for head in range(HEADS):
        low, high = head * HEAD_DIM, (head + 1) * HEAD_DIM
        first, last = low // 128, (high - 1) // 128
        window = slice(first * 128, (last + 1) * 128)
        lane = lax.broadcasted_iota(jnp.int32, (count, window.stop - window.start), 1)
        lane = lane + window.start
        inside = jnp.logical_and(lane >= low, lane < high)
        queries = jnp.where(inside, qk[0, rows, window], jnp.zeros((), BF16))
        keys = jnp.where(inside, qk[1, rows, window], jnp.zeros((), BF16))
        scores = lax.dot_general(
            queries, keys, (((1,), (1,)), ((), ())), preferred_element_type=F32
        )
        weights = jnp.exp2(scores)
        if mask is not None:
            weights = jnp.where(mask, weights, 0.0)
        weights = weights.astype(BF16)
        total = jnp.dot(weights, ones, preferred_element_type=F32)
        inverse = 1.0 / total
        for t in range(first, last + 1):
            mixed = jnp.dot(
                weights, vals[rows, t * 128 : (t + 1) * 128], preferred_element_type=F32
            )
            mixed = mixed * inverse
            if tiles[t] is None:
                tiles[t] = mixed
            else:
                at = lax.broadcasted_iota(jnp.int32, mixed.shape, 1) + t * 128
                tiles[t] = jnp.where(at >= low, mixed, tiles[t])
    return tiles


def kernel(
    lat_hbm, time_ref, size_ref, mod_hbm, w1_hbm, o1_hbm, w2_hbm, o2_hbm,
    out_hbm, change_ref,
    lat, mod, w1, o1, w2, o2, member, spread, qk, vals, heads, cond,
    following, after, anchor, mine, drift, x_in, total, z_in, carry, c_in, done, u_in, out,
    part, parts,
    local_sem, next_send, next_recv, anchor_send, anchor_recv, y_send, y_recv,
    x_send, x_recv, z_send, z_recv, c_send, c_recv, u_send, u_recv, p_send, p_recv, out_sem,
):
    me = lax.axis_index("step")
    s = lax.axis_index("seq")
    z, x = me // NX, lax.rem(me, NX)
    rp, cg = x // 2, lax.rem(x, 2)

    loads = [
        pltpu.make_async_copy(src, dst, local_sem.at[i])
        for i, (src, dst) in enumerate(
            [(lat_hbm, lat), (mod_hbm, mod), (w1_hbm, w1), (o1_hbm, o1), (w2_hbm, w2), (o2_hbm, o2)]
        )
    ]
    for load in loads:
        load.start()

    def to(step, seq):
        return {"step": step, "seq": seq}

    barrier = pltpu.get_barrier_semaphore()
    before = lax.rem(me + NX * NZ - 1, NX * NZ)
    behind = lax.rem(me + 1, NX * NZ)

    def greet_plane(k, _):
        other_s = lax.rem(s + lax.rem(k, NS), NS)
        other_x = lax.rem(x + k // NS, NX)
        pl.semaphore_signal(barrier, inc=1, device_id=to(z * NX + other_x, other_s), device_id_type=MESH)
        return _

    lax.fori_loop(1, NX * NS, greet_plane, 0)

    def greet_planes(k, _):
        other_z = lax.rem(z + k, NZ)
        pl.semaphore_signal(barrier, inc=1, device_id=to(other_z * NX + x, s), device_id_type=MESH)
        return _

    lax.fori_loop(1, NZ, greet_planes, 0)
    for step in (before, behind):
        pl.semaphore_signal(barrier, inc=1, device_id=to(step, s), device_id_type=MESH)

    column = lax.broadcasted_iota(jnp.int32, (2 * E, 128), 0)
    head = lax.broadcasted_iota(jnp.int32, (2 * E, 128), 1) * HEAD_DIM
    member[...] = jnp.where(
        jnp.logical_and(column >= head, column < head + HEAD_DIM), 1.0, 0.0
    ).astype(BF16)
    column = lax.broadcasted_iota(jnp.int32, (256, 2 * E), 1)
    head = lax.rem(lax.broadcasted_iota(jnp.int32, (256, 2 * E), 0), 128) * HEAD_DIM
    spread[...] = jnp.where(
        jnp.logical_and(column >= head, column < head + HEAD_DIM), 1.0, 0.0
    ).astype(BF16)

    loads[1].wait()
    one_hot = (lax.broadcasted_iota(jnp.int32, (16, mod.shape[0]), 1) == time_ref[0]).astype(BF16)
    cond[...] = jnp.dot(one_hot, mod[...], preferred_element_type=F32)

    def vector(i):
        return cond[0:1, i * D : (i + 1) * D]

    loads[0].wait()
    spatial_in = (layer_norm(lat[...].astype(F32)) * (1.0 + vector(1)) + vector(0)).astype(BF16)

    pl.semaphore_wait(barrier, NX * NS - 1 + NZ - 1 + 2)
    send_next = pltpu.make_async_remote_copy(
        src_ref=lat, dst_ref=following, send_sem=next_send, recv_sem=next_recv,
        device_id=to(before, s), device_id_type=MESH,
    )
    send_next.start()

    def piece(k, half):
        return pl.ds(pl.multiple_of(half * HALF + k * PIECE, PIECE), PIECE)

    def y_copy(src, dst, send, recv, k, half, sender, target):
        return pltpu.make_async_remote_copy(
            src_ref=src.at[piece(target, half), :], dst_ref=dst.at[piece(sender, half), :],
            send_sem=send.at[half, k], recv_sem=recv.at[half, sender],
            device_id=to(me, target), device_id_type=MESH,
        )

    def y_start(src, dst, send, recv):
        def start(k, _):
            for half in range(2):
                y_copy(src, dst, send, recv, k, half, s, lax.rem(s + k, NS)).start()
            return _

        lax.fori_loop(1, NS, start, 0)

    def y_wait(src, dst, send, recv, arrived):
        def wait(k, _):
            for half in range(2):
                copy = y_copy(src, dst, send, recv, k, half, lax.rem(s + k, NS), s)
                if arrived:
                    copy.wait_recv()
                else:
                    copy.wait_send()
            return _

        lax.fori_loop(1, NS, wait, 0)

    def keep_own(src, dst):
        for half in range(2):
            dst[piece(s, half), :] = src[piece(s, half), :]

    @pl.when(me == 0)
    def _():
        y_start(lat, anchor, anchor_send, anchor_recv)
        keep_own(lat, anchor)

    def put_heads(rows, tiles):
        for t in range(4):
            heads[rows, t * 128 : (t + 1) * 128] = tiles[t].astype(BF16)
        heads[rows, 512:E] = tiles[4][:, : E - 512].astype(BF16)

    loads[2].wait()
    project(spatial_in, w1, member, spread, qk, vals)
    everything = pl.ds(0, ROWS)
    put_heads(everything, attend(qk, vals, everything, None))
    loads[3].wait()
    after[...] = (
        lat[...].astype(F32) + vector(2) * jnp.dot(heads[...], o1[...], preferred_element_type=F32)
    ).astype(BF16)

    y_start(after, mine, y_send, y_recv)
    keep_own(after, mine)
    loads[4].wait()
    loads[5].wait()
    y_wait(after, mine, y_send, y_recv, True)

    own = mine[...].astype(F32)
    temporal_in = (layer_norm(own) * (1.0 + vector(4)) + vector(3)).astype(BF16)
    project(temporal_in, w2, member, spread, qk, vals)
    patch = lax.rem(lax.broadcasted_iota(jnp.int32, (HALF, HALF), 0), PIECE)
    patch_of_key = lax.rem(lax.broadcasted_iota(jnp.int32, (HALF, HALF), 1), PIECE)
    for half in range(2):
        rows = pl.ds(half * HALF, HALF)
        put_heads(rows, attend(qk, vals, rows, patch == patch_of_key))
    term = size_ref[0] * (
        mine[...].astype(F32) + vector(5) * jnp.dot(heads[...], o2[...], preferred_element_type=F32)
    )
    drift[...] = term.astype(BF16)

    @pl.when(me == 0)
    def _():
        y_wait(lat, anchor, anchor_send, anchor_recv, True)
        drift[...] = (drift[...].astype(F32) + anchor[...].astype(F32)).astype(BF16)

    def block(holder):
        row = pl.multiple_of((holder // 2) * HALF, HALF)
        col = pl.multiple_of(lax.rem(holder, 2) * SHIFT, 128)
        return pl.ds(row, HALF), pl.ds(col, WIDE)

    def x_copy(k, sender, target):
        rows, cols = block(target)
        return pltpu.make_async_remote_copy(
            src_ref=drift.at[rows, cols], dst_ref=x_in.at[sender],
            send_sem=x_send.at[k], recv_sem=x_recv.at[sender],
            device_id=to(z * NX + target, s), device_id_type=MESH,
        )

    for k in range(1, NX):
        x_copy(k, x, lax.rem(x + k, NX)).start()
    rows, cols = block(x)
    x_in[x] = drift[rows, cols]
    for k in range(1, NX):
        x_copy(k, lax.rem(x + k, NX), x).wait_recv()
    total[...] = (
        x_in[0].astype(F32) + x_in[1].astype(F32) + x_in[2].astype(F32) + x_in[3].astype(F32)
    ).astype(BF16).reshape(NZ, PIECE, WIDE)

    def z_copy(k, sender, target):
        return pltpu.make_async_remote_copy(
            src_ref=total.at[target], dst_ref=z_in.at[sender],
            send_sem=z_send.at[k], recv_sem=z_recv.at[sender],
            device_id=to(target * NX + x, s), device_id_type=MESH,
        )

    def c_copy(k, sender, target):
        return pltpu.make_async_remote_copy(
            src_ref=carry.at[target], dst_ref=c_in.at[sender],
            send_sem=c_send.at[k], recv_sem=c_recv.at[sender],
            device_id=to(target * NX + x, s), device_id_type=MESH,
        )

    for k in range(1, NZ):
        z_copy(k, z, lax.rem(z + k, NZ)).start()
    z_in[z] = total[z]
    for k in range(1, NZ):
        z_copy(k, lax.rem(z + k, NZ), z).wait_recv()
    running = jnp.zeros((PIECE, WIDE), F32)
    for k in range(NZ):
        carry[k] = running.astype(BF16)
        running = running + z_in[k].astype(F32)
    for k in range(1, NZ):
        c_copy(k, z, lax.rem(z + k, NZ)).start()
    c_in[z] = carry[z]
    for k in range(1, NZ):
        c_copy(k, lax.rem(z + k, NZ), z).wait_recv()

    running = c_in[...].astype(F32).reshape(HALF, WIDE)
    for k in range(NX):
        running = running + x_in[k].astype(F32)
        done[k] = running.astype(BF16).reshape(NS, PIECE, WIDE)

    def u_copy(k, x_from, s_from, x_to, s_to):
        row = pl.multiple_of((x_from // 2) * HALF + s_from * PIECE, PIECE)
        return pltpu.make_async_remote_copy(
            src_ref=done.at[x_to, s_to],
            dst_ref=u_in.at[lax.rem(x_from, 2), pl.ds(row, PIECE), :],
            send_sem=u_send.at[k], recv_sem=u_recv.at[x_from, s_from],
            device_id=to(z * NX + x_to, s_to), device_id_type=MESH,
        )

    def u_start(k, _):
        u_copy(k, x, s, lax.rem(x + k // NS, NX), lax.rem(s + lax.rem(k, NS), NS)).start()
        return _

    def u_wait(k, _):
        u_copy(k, lax.rem(x + k // NS, NX), lax.rem(s + lax.rem(k, NS), NS), x, s).wait_recv()
        return _

    lax.fori_loop(1, NX * NS, u_start, 0)
    u_in[cg, piece(s, rp), :] = done[x, s]
    send_next.wait_recv()
    lax.fori_loop(1, NX * NS, u_wait, 0)

    out[:, :WIDE] = u_in[0]
    out[:, WIDE:] = u_in[1, :, 128:]
    store = pltpu.make_async_copy(out, out_hbm, out_sem)
    store.start()
    known = jnp.where(me == NX * NZ - 1, 0.0, 1.0)
    after_this = jnp.where(known > 0.5, following[...].astype(F32), 0.0)
    difference = out[...].astype(F32) - after_this
    squares = (difference * difference).reshape(ROWS // 8, 8, D).sum(axis=0)
    tile = squares[:, :128]
    for t in range(1, D // 128):
        tile = tile + squares[:, t * 128 : (t + 1) * 128]
    part[...] = tile

    def p_copy(k, sender, target):
        return pltpu.make_async_remote_copy(
            src_ref=part, dst_ref=parts.at[sender],
            send_sem=p_send.at[k], recv_sem=p_recv.at[sender],
            device_id=to(me, target), device_id_type=MESH,
        )

    for k in range(1, NS):
        p_copy(k, s, lax.rem(s + k, NS)).start()
    parts[s] = part[...]
    for k in range(1, NS):
        p_copy(k, lax.rem(s + k, NS), s).wait_recv()
    change_ref[0] = jnp.sum(jnp.sum(parts[...], axis=0)) * (1.0 / (NS * ROWS * D))

    send_next.wait_send()

    @pl.when(me == 0)
    def _():
        y_wait(lat, anchor, anchor_send, anchor_recv, False)

    y_wait(after, mine, y_send, y_recv, False)
    for k in range(1, NX):
        x_copy(k, x, lax.rem(x + k, NX)).wait_send()
    for k in range(1, NZ):
        z_copy(k, z, lax.rem(z + k, NZ)).wait_send()
        c_copy(k, z, lax.rem(z + k, NZ)).wait_send()

    def u_left(k, _):
        u_copy(k, x, s, lax.rem(x + k // NS, NX), lax.rem(s + lax.rem(k, NS), NS)).wait_send()
        return _

    lax.fori_loop(1, NX * NS, u_left, 0)
    for k in range(1, NS):
        p_copy(k, s, lax.rem(s + k, NS)).wait_send()
    store.wait()


def body(latents, timesteps, step_sizes, modulation, spatial_qkv, spatial_out, temporal_qkv, temporal_out):
    dma = pltpu.SemaphoreType.DMA
    anywhere = pl.BlockSpec(memory_space=pl.ANY)
    scalar = pl.BlockSpec(memory_space=pltpu.SMEM)

    def vmem(*shape, dtype=BF16):
        return pltpu.VMEM(shape, dtype)

    table = modulation.shape[0]
    updated, change = pl.pallas_call(
        kernel,
        out_shape=(jax.ShapeDtypeStruct((ROWS, D), BF16), jax.ShapeDtypeStruct((1,), F32)),
        in_specs=[anywhere, scalar, scalar] + [anywhere] * 5,
        out_specs=(anywhere, scalar),
        scratch_shapes=[
            vmem(ROWS, D), vmem(table, 6 * D),
            vmem(D, 3 * E), vmem(E, D), vmem(D, 3 * E), vmem(E, D),
            vmem(2 * E, 128), vmem(256, 2 * E),
            vmem(2, ROWS, 640), vmem(ROWS, 640), vmem(ROWS, E), vmem(16, 6 * D, dtype=F32),
            vmem(ROWS, D), vmem(ROWS, D), vmem(ROWS, D), vmem(ROWS, D), vmem(ROWS, D),
            vmem(NX, HALF, WIDE), vmem(NZ, PIECE, WIDE), vmem(NZ, PIECE, WIDE),
            vmem(NZ, PIECE, WIDE), vmem(NZ, PIECE, WIDE),
            vmem(NX, NS, PIECE, WIDE), vmem(2, ROWS, WIDE), vmem(ROWS, D),
            vmem(8, 128, dtype=F32), vmem(NS, 8, 128, dtype=F32),
            dma((6,)), dma, dma, dma((2, NS)), dma((2, NS)), dma((2, NS)), dma((2, NS)),
            dma((NX,)), dma((NX,)), dma((NZ,)), dma((NZ,)), dma((NZ,)), dma((NZ,)),
            dma((NX * NS,)), dma((NX, NS)), dma((NS,)), dma((NS,)), dma,
        ],
        compiler_params=pltpu.CompilerParams(
            collective_id=0, has_side_effects=True, vmem_limit_bytes=48 * 1024 * 1024
        ),
        cost_estimate=pl.CostEstimate(
            flops=2800000000, bytes_accessed=12000000, transcendentals=1000000
        ),
    )(
        latents.reshape(ROWS, D), timesteps, step_sizes, modulation,
        spatial_qkv, spatial_out, temporal_qkv, temporal_out,
    )
    return updated[None, None], change


def solution(mesh):
    in_specs = (P("step", "seq", None, None), P("step"), P("step"), P(), P(), P(), P(), P())
    out_specs = (P("step", "seq", None, None), P("step"))
    return jax.shard_map(body, mesh=mesh, in_specs=in_specs, out_specs=out_specs, check_vma=False)
```

time: 414 us -> 89.4 us (0.22)
  the two profiles are of different devices: /device:TPU:33 before, /device:TPU:1 now
where the time goes in v1:
time: 89.4 us; the launch traced here: 89 us
  Pallas kernels  70.4 us (79%)
  local copies, waits for them, and re-layouts  14.9 us (17%)
  between operations  3.71 us (4%)
    pallas_call x1, Pallas kernels, body(): pl.pallas_call(kernel, out_shape=(jax.ShapeDtypeStruct((ROWS, D), BF16),...  70.4 us
    unnamed x11, local copies, waits for them, and re-layouts  14.9 us

profile of v1, /device:TPU:1, one launch (start us, length us, event | category | flops | bytes accessed | tf_op | source)
XLA Modules:
  0.0 89.0 jit_solution(11575278529222031543)
XLA Ops:
  1.9 6.4 %copy.10.w1_hbm = bf16[1152,1728]{1,0:T(8,128)(2,1)} copy(bf16[1152,1728]{0,1:T(8,128)(2,1)} %param.12) | data formatting | bytes 7962624 | tf_op args[4]
  8.4 0.0 copy-start
  8.4 0.0 copy-start.1
  8.4 0.0 copy-start.2
  8.4 6.6 %copy.11.w2_hbm = bf16[1152,1728]{1,0:T(8,128)(2,1)} copy(bf16[1152,1728]{0,1:T(8,128)(2,1)} %param.14) | data formatting | bytes 7962624 | tf_op args[6]
  15.0 0.0 copy-done
  15.0 0.0 copy-done.1
  15.0 0.0 copy-done.2
  15.0 0.0 copy-start.3
  15.0 1.0 %copy-done.3 = bf16[32,6912]{1,0:T(8,128)(2,1)S(1)} copy-done((bf16[32,6912]{1,0:T(8,128)(2,1)S(1)}, bf16[32,6912]{1,0:T(8,128)(2,1)}, u32[]{:S(2)}) %copy-start.3) | copy-done | bytes 442392
  16.0 70.4 %shard_map.95 = (bf16[256,1152]{1,0:T(8,128)(2,1)S(1)}, f32[1]{0:T(128)}) custom-call(bf16[256,1152]{1,0:T(8,128)(2,1)S(1)} %bitcast.2, s32[1]{0:T(128)S(6)} %copy.14.time_ref, f32[1]{0:T(128)S(6)} %copy.15.size_ref, bf16[32,6912]{1,0:T(8,128)(2,1)S(1)} %copy-done.3, bf16[1152,1728]{1,0:T(8,128)(2,1)} %copy.10.w1_hbm, bf16[576,1152]{1,0:T(8,128)(2,1)S(1)} %copy-done, ...), custom_call_target="tpu_custom_call" | custom-call | flops 2800000000 | bytes 12000000 | tf_op jit(solution)/shard_map/pallas_call | solution.py:379
  86.5 0.8 copy.16
Async XLA Ops:
  8.4 6.6 %copy-start = (bf16[576,1152]{1,0:T(8,128)(2,1)S(1)}, bf16[576,1152]{1,0:T(8,128)(2,1)}, u32[]{:S(2)}) copy-start(bf16[576,1152]{1,0:T(8,128)(2,1)} %o1_hbm.1) | copy-start | bytes 3981316
  8.4 6.6 %copy-start.1 = (bf16[576,1152]{1,0:T(8,128)(2,1)S(1)}, bf16[576,1152]{1,0:T(8,128)(2,1)}, u32[]{:S(2)}) copy-start(bf16[576,1152]{1,0:T(8,128)(2,1)} %o2_hbm.1) | copy-start | bytes 3981316
  8.4 6.6 %copy-start.2 = (bf16[1,1,256,1152]{3,2,1,0:T(8,128)(2,1)S(1)}, bf16[1,1,256,1152]{3,2,1,0:T(8,128)(2,1)}, u32[]{:S(2)}) copy-start(bf16[1,1,256,1152]{3,2,1,0:T(8,128)(2,1)} %param.8) | copy-start | bytes 1769476
  15.0 1.0 %copy-start.3 = (bf16[32,6912]{1,0:T(8,128)(2,1)S(1)}, bf16[32,6912]{1,0:T(8,128)(2,1)}, u32[]{:S(2)}) copy-start(bf16[32,6912]{1,0:T(8,128)(2,1)} %mod_hbm.1) | copy-start | bytes 1327108

commit v2 on v1

v2 whole, which is shorter than its diff:
```python
import math

import jax
import jax.numpy as jnp
from jax import lax
from jax.experimental import pallas as pl
from jax.experimental.pallas import tpu as pltpu
from jax.sharding import PartitionSpec as P

UNROLL = 8
MESH = pl.DeviceIdType.MESH
F32 = jnp.float32
BF16 = jnp.bfloat16

D = 1152
HEADS = 8
HEAD_DIM = 72
E = HEADS * HEAD_DIM
ROWS = 256
HALF = 128
PIECE = 16
NX = 4
NZ = 8
NS = 8
QUART = 64
WIDE = 640
SHIFT = 512
EPS = 1e-6
LOG2E = 1.4426950408889634
Q_SCALE = 3.0 / math.sqrt(HEAD_DIM) * LOG2E


def layer_norm(values):
    center = values - jnp.mean(values, axis=-1, keepdims=True)
    spread = jnp.mean(center * center, axis=-1, keepdims=True)
    return center * lax.rsqrt(spread + EPS)


def attend(raw, heads, queries, mask):
    def unit(rows, columns, scale):
        values = raw[rows, columns]
        squares = jnp.sum(values * values, axis=0, keepdims=True)
        return (values * (lax.rsqrt(squares * (1.0 / HEAD_DIM) + EPS) * scale)).astype(BF16)

    def one_head(head, _):
        first = [pl.multiple_of(i * E + head * HEAD_DIM, 8) for i in range(3)]
        asked = unit(pl.ds(first[0], HEAD_DIM), queries, Q_SCALE)
        keys = unit(pl.ds(first[1], HEAD_DIM), slice(None), 1.0)
        scores = lax.dot_general(keys, asked, (((0,), (0,)), ((), ())), preferred_element_type=F32)
        weights = jnp.exp2(scores)
        if mask is not None:
            weights = jnp.where(mask, weights, 0.0)
        inverse = 1.0 / jnp.sum(weights, axis=0, keepdims=True)
        values = raw[pl.ds(first[2], HEAD_DIM), :].astype(BF16)
        mixed = jnp.dot(values, weights.astype(BF16), preferred_element_type=F32)
        heads[pl.ds(first[0], HEAD_DIM), :] = mixed * inverse
        return _

    lax.fori_loop(0, HEADS, one_head, 0, unroll=UNROLL)


def kernel(
    lat_hbm, time_ref, size_ref, mod_hbm, w1_hbm, o1_hbm, w2_hbm, o2_hbm,
    out_hbm, change_ref,
    lat, mod, w1, o1, w2, o2, cond, inputs, raw, raw_half, heads,
    following, after, anchor, mine, drift, x_in, total, z_in, carry, c_in, done, u_in, out,
    part, parts,
    local_sem, next_send, next_recv, anchor_send, anchor_recv, y_send, y_recv,
    x_send, x_recv, z_send, z_recv, c_send, c_recv, u_send, u_recv, p_send, p_recv, out_sem,
):
    me = lax.axis_index("step")
    s = lax.axis_index("seq")
    z, x = me // NX, lax.rem(me, NX)
    fh, cg = x // 2, lax.rem(x, 2)

    loads = [
        pltpu.make_async_copy(src, dst, local_sem.at[i])
        for i, (src, dst) in enumerate(
            [(lat_hbm, lat), (mod_hbm, mod), (w1_hbm, w1), (o1_hbm, o1), (w2_hbm, w2), (o2_hbm, o2)]
        )
    ]
    for load in loads:
        load.start()

    def to(step, seq):
        return {"step": step, "seq": seq}

    barrier = pltpu.get_barrier_semaphore()
    before = lax.rem(me + NX * NZ - 1, NX * NZ)
    behind = lax.rem(me + 1, NX * NZ)

    def greet_plane(k, _):
        other_s = lax.rem(s + lax.rem(k, NS), NS)
        other_x = lax.rem(x + k // NS, NX)
        pl.semaphore_signal(barrier, inc=1, device_id=to(z * NX + other_x, other_s), device_id_type=MESH)
        return _

    lax.fori_loop(1, NX * NS, greet_plane, 0)

    def greet_planes(k, _):
        other_z = lax.rem(z + k, NZ)
        pl.semaphore_signal(barrier, inc=1, device_id=to(other_z * NX + x, s), device_id_type=MESH)
        return _

    lax.fori_loop(1, NZ, greet_planes, 0)
    for step in (before, behind):
        pl.semaphore_signal(barrier, inc=1, device_id=to(step, s), device_id_type=MESH)

    loads[1].wait()
    one_hot = (lax.broadcasted_iota(jnp.int32, (16, mod.shape[0]), 1) == time_ref[0]).astype(BF16)
    cond[...] = jnp.dot(one_hot, mod[...], preferred_element_type=F32)[:8]

    def vector(i):
        return cond[0:1, i * D : (i + 1) * D]

    def condition(src, start, count, shift, scale):
        def some(i, _):
            rows = pl.ds(pl.multiple_of(start + i * PIECE, PIECE), PIECE)
            normal = layer_norm(src[rows, :].astype(F32))
            inputs[rows, :] = (normal * (1.0 + vector(scale)) + vector(shift)).astype(BF16)
            return _

        lax.fori_loop(0, count // PIECE, some, 0, unroll=2)

    def piece(k, half):
        return pl.ds(pl.multiple_of(half * HALF + k * PIECE, PIECE), PIECE)

    def y_copy(src, dst, send, recv, k, half, sender, target):
        return pltpu.make_async_remote_copy(
            src_ref=src.at[piece(target, half), :], dst_ref=dst.at[piece(sender, half), :],
            send_sem=send.at[half, k], recv_sem=recv.at[half, sender],
            device_id=to(me, target), device_id_type=MESH,
        )

    def y_start(src, dst, send, recv, half):
        def start(k, _):
            y_copy(src, dst, send, recv, k, half, s, lax.rem(s + k, NS)).start()
            return _

        lax.fori_loop(1, NS, start, 0)
        dst[piece(s, half), :] = src[piece(s, half), :]

    def y_wait(src, dst, send, recv, half, arrived):
        def wait(k, _):
            copy = y_copy(src, dst, send, recv, k, half, lax.rem(s + k, NS), s)
            if arrived:
                copy.wait_recv()
            else:
                copy.wait_send()
            return _

        lax.fori_loop(1, NS, wait, 0)

    loads[0].wait()
    condition(lat, 0, ROWS, 0, 1)
    pl.semaphore_wait(barrier, NX * NS - 1 + NZ - 1 + 2)

    @pl.when(me == 0)
    def _():
        for half in range(2):
            y_start(lat, anchor, anchor_send, anchor_recv, half)

    send_next = pltpu.make_async_remote_copy(
        src_ref=lat, dst_ref=following, send_sem=next_send, recv_sem=next_recv,
        device_id=to(before, s), device_id_type=MESH,
    )
    send_next.start()

    contract_last = (((1,), (1,)), ((), ()))
    contract_first = (((0,), (0,)), ((), ()))
    halves = [slice(half * HALF, (half + 1) * HALF) for half in range(2)]

    loads[2].wait()
    raw[...] = lax.dot_general(w1[...], inputs[...], contract_last, preferred_element_type=F32)
    for half in range(2):
        rows = halves[half]
        attend(raw, heads, rows, None)
        if half == 0:
            loads[3].wait()
        shown = lax.dot_general(heads[...].astype(BF16), o1[...], contract_first, preferred_element_type=F32)
        after[rows, :] = (lat[rows, :].astype(F32) + vector(2) * shown).astype(BF16)
        y_start(after, mine, y_send, y_recv, half)
    loads[4].wait()
    loads[5].wait()

    def block(half, holder):
        row = pl.multiple_of(half * HALF + (holder // 2) * QUART, QUART)
        col = pl.multiple_of(lax.rem(holder, 2) * SHIFT, 128)
        return pl.ds(row, QUART), pl.ds(col, WIDE)

    def x_copy(half, k, sender, target):
        rows, cols = block(half, target)
        return pltpu.make_async_remote_copy(
            src_ref=drift.at[rows, cols], dst_ref=x_in.at[half, sender],
            send_sem=x_send.at[half, k], recv_sem=x_recv.at[half, sender],
            device_id=to(z * NX + target, s), device_id_type=MESH,
        )

    patch = lax.rem(lax.broadcasted_iota(jnp.int32, (HALF, HALF), 0), PIECE)
    patch_of_key = lax.rem(lax.broadcasted_iota(jnp.int32, (HALF, HALF), 1), PIECE)
    for half in range(2):
        rows = halves[half]
        y_wait(after, mine, y_send, y_recv, half, True)
        condition(mine, half * HALF, HALF, 3, 4)
        raw_half[...] = lax.dot_general(w2[...], inputs[rows, :], contract_last, preferred_element_type=F32)
        attend(raw_half, heads, slice(None), patch == patch_of_key)
        shown = lax.dot_general(heads[...].astype(BF16), o2[...], contract_first, preferred_element_type=F32)
        drift[rows, :] = (size_ref[0] * (mine[rows, :].astype(F32) + vector(5) * shown)).astype(BF16)

        @pl.when(me == 0)
        def _():
            y_wait(lat, anchor, anchor_send, anchor_recv, half, True)
            drift[rows, :] = (drift[rows, :].astype(F32) + anchor[rows, :].astype(F32)).astype(BF16)

        for k in range(1, NX):
            x_copy(half, k, x, lax.rem(x + k, NX)).start()
        own_rows, own_cols = block(half, x)
        x_in[half, x] = drift[own_rows, own_cols]

    def z_copy(half, frame, sender, target):
        return pltpu.make_async_remote_copy(
            src_ref=total.at[half, frame], dst_ref=z_in.at[sender],
            send_sem=z_send.at[half, frame], recv_sem=z_recv.at[sender],
            device_id=to(target * NX + x, s), device_id_type=MESH,
        )

    for half in range(2):
        for k in range(1, NX):
            x_copy(half, k, lax.rem(x + k, NX), x).wait_recv()
        block_sum = x_in[half, 0].astype(F32)
        for k in range(1, NX):
            block_sum = block_sum + x_in[half, k].astype(F32)
        total[half] = block_sum.astype(BF16).reshape(NX, PIECE, WIDE)
        for frame in range(4):
            target = 2 * frame + half

            @pl.when(z != target)
            def _():
                z_copy(half, frame, z, target).start()

            @pl.when(z == target)
            def _():
                z_in[z] = total[half, frame]

    def c_copy(half, k, holder, target):
        return pltpu.make_async_remote_copy(
            src_ref=carry.at[target], dst_ref=c_in.at[half, holder // 2],
            send_sem=c_send.at[k], recv_sem=c_recv.at[half, holder // 2],
            device_id=to(target * NX + x, s), device_id_type=MESH,
        )

    for half in range(2):

        @pl.when(lax.rem(z, 2) == half)
        def _():
            for k in range(1, NZ):
                z_copy(half, 0, lax.rem(z + k, NZ), z).wait_recv()
            running = jnp.zeros((PIECE, WIDE), F32)
            for k in range(NZ):
                carry[k] = running.astype(BF16)
                running = running + z_in[k].astype(F32)
            for k in range(1, NZ):
                c_copy(half, k, z, lax.rem(z + k, NZ)).start()
            c_in[half, z // 2] = carry[z]

    def u_copy(half, k, x_from, s_from, x_to, frame):
        return pltpu.make_async_remote_copy(
            src_ref=done.at[half, x_to, frame],
            dst_ref=u_in.at[lax.rem(x_from, 2), piece(s_from, half), :],
            send_sem=u_send.at[half, k], recv_sem=u_recv.at[half, lax.rem(x_from, 2), s_from],
            device_id=to(z * NX + x_to, (x_from // 2) * 4 + frame), device_id_type=MESH,
        )

    def u_each(half, do):
        def step(k, held):
            x_to, frame = lax.rem(x + k // 4, NX), lax.rem(k, 4)
            copy = u_copy(half, k, x, s, x_to, frame)

            @pl.when(jnp.logical_or(x_to != x, fh * 4 + frame != s))
            def _():
                do(copy)

            return held

        lax.fori_loop(0, NX * 4, step, 0)

    for half in range(2):
        for frame in range(4):

            @pl.when(z != 2 * frame + half)
            def _():
                c_copy(half, 0, 2 * frame + half, z).wait_recv()

        running = c_in[half].astype(F32).reshape(QUART, WIDE)
        for k in range(NX):
            running = running + x_in[half, k].astype(F32)
            done[half, k] = running.astype(BF16).reshape(4, PIECE, WIDE)
        u_each(half, lambda copy: copy.start())

        @pl.when(s // 4 == fh)
        def _():
            u_in[cg, piece(s, half), :] = done[half, x, lax.rem(s, 4)]

    send_next.wait_recv()
    known = jnp.where(me == NX * NZ - 1, 0.0, 1.0)
    part[...] = jnp.zeros_like(part)
    stores = []
    for half in range(2):
        rows = halves[half]

        def arrive(k, held):
            group, sender = k // NS, lax.rem(k, NS)
            x_from = (s // 4) * 2 + group

            @pl.when(jnp.logical_or(x_from != x, sender != s))
            def _():
                u_copy(half, 0, x_from, sender, x, lax.rem(s, 4)).wait_recv()

            return held

        lax.fori_loop(0, 2 * NS, arrive, 0)
        out[rows, :WIDE] = u_in[0, rows, :]
        out[rows, WIDE:] = u_in[1, rows, 128:]
        store = pltpu.make_async_copy(out.at[rows, :], out_hbm.at[rows, :], out_sem.at[half])
        store.start()
        stores.append(store)
        goal = jnp.where(known > 0.5, following[rows, :].astype(F32), 0.0)
        difference = out[rows, :].astype(F32) - goal
        squares = (difference * difference).reshape(HALF // 8, 8, D).sum(axis=0)
        for t in range(D // 128):
            part[...] += squares[:, t * 128 : (t + 1) * 128]

    def p_copy(k, sender, target):
        return pltpu.make_async_remote_copy(
            src_ref=part, dst_ref=parts.at[sender],
            send_sem=p_send.at[k], recv_sem=p_recv.at[sender],
            device_id=to(me, target), device_id_type=MESH,
        )

    for k in range(1, NS):
        p_copy(k, s, lax.rem(s + k, NS)).start()
    parts[s] = part[...]
    for k in range(1, NS):
        p_copy(k, lax.rem(s + k, NS), s).wait_recv()
    change_ref[0] = jnp.sum(jnp.sum(parts[...], axis=0)) * (1.0 / (NS * ROWS * D))

    send_next.wait_send()
    for half in range(2):

        @pl.when(me == 0)
        def _():
            y_wait(lat, anchor, anchor_send, anchor_recv, half, False)

        y_wait(after, mine, y_send, y_recv, half, False)
        for k in range(1, NX):
            x_copy(half, k, x, lax.rem(x + k, NX)).wait_send()
        for frame in range(4):

            @pl.when(z != 2 * frame + half)
            def _():
                z_copy(half, frame, z, 2 * frame + half).wait_send()

        u_each(half, lambda copy: copy.wait_send())
    for k in range(1, NZ):
        c_copy(0, k, z, lax.rem(z + k, NZ)).wait_send()
    for k in range(1, NS):
        p_copy(k, s, lax.rem(s + k, NS)).wait_send()
    for store in stores:
        store.wait()


def body(latents, timesteps, step_sizes, modulation, spatial_qkv, spatial_out, temporal_qkv, temporal_out):
    dma = pltpu.SemaphoreType.DMA
    anywhere = pl.BlockSpec(memory_space=pl.ANY)
    scalar = pl.BlockSpec(memory_space=pltpu.SMEM)

    def vmem(*shape, dtype=BF16):
        return pltpu.VMEM(shape, dtype)

    table = modulation.shape[0]
    updated, change = pl.pallas_call(
        kernel,
        out_shape=(jax.ShapeDtypeStruct((ROWS, D), BF16), jax.ShapeDtypeStruct((1,), F32)),
        in_specs=[anywhere, scalar, scalar] + [anywhere] * 5,
        out_specs=(anywhere, scalar),
        scratch_shapes=[
            vmem(ROWS, D), vmem(table, 6 * D),
            vmem(3 * E, D), vmem(E, D), vmem(3 * E, D), vmem(E, D),
            vmem(8, 6 * D, dtype=F32), vmem(ROWS, D),
            vmem(3 * E, ROWS, dtype=F32), vmem(3 * E, HALF, dtype=F32), vmem(E, HALF, dtype=F32),
            vmem(ROWS, D), vmem(ROWS, D), vmem(ROWS, D), vmem(ROWS, D), vmem(ROWS, D),
            vmem(2, NX, QUART, WIDE), vmem(2, 4, PIECE, WIDE), vmem(NZ, PIECE, WIDE),
            vmem(NZ, PIECE, WIDE), vmem(2, 4, PIECE, WIDE),
            vmem(2, NX, 4, PIECE, WIDE), vmem(2, ROWS, WIDE), vmem(ROWS, D),
            vmem(8, 128, dtype=F32), vmem(NS, 8, 128, dtype=F32),
            dma((6,)), dma, dma, dma((2, NS)), dma((2, NS)), dma((2, NS)), dma((2, NS)),
            dma((2, NX)), dma((2, NX)), dma((2, 4)), dma((NZ,)), dma((NZ,)), dma((2, 4)),
            dma((2, NX * 4)), dma((2, 2, NS)), dma((NS,)), dma((NS,)), dma((2,)),
        ],
        compiler_params=pltpu.CompilerParams(
            collective_id=0, has_side_effects=True, vmem_limit_bytes=56 * 1024 * 1024
        ),
        cost_estimate=pl.CostEstimate(
            flops=2800000000, bytes_accessed=12000000, transcendentals=1000000
        ),
    )(
        latents.reshape(ROWS, D), timesteps, step_sizes, modulation,
        spatial_qkv.T, spatial_out, temporal_qkv.T, temporal_out,
    )
    return updated[None, None], change


def solution(mesh):
    in_specs = (P("step", "seq", None, None), P("step"), P("step"), P(), P(), P(), P(), P())
    out_specs = (P("step", "seq", None, None), P("step"))
    return jax.shard_map(body, mesh=mesh, in_specs=in_specs, out_specs=out_specs, check_vma=False)
```

time: 89.4 us -> 69.1 us (0.77)
  local copies, waits for them, and re-layouts: 14.9 us -> 1.92 us
  Pallas kernels: 70.4 us -> 63.2 us
    unnamed x11 -> x1, local copies, waits for them, and re-layouts: 14.9 us -> 1.92 us
    pallas_call x1, Pallas kernels: 70.4 us -> 63.2 us  [body(): pl.pallas_call(kernel, out_shape=(jax.ShapeDtypeStruct((ROWS, D), BF16),...]
where the time goes in v2:
time: 69.1 us; the launch traced here: 68.9 us
  Pallas kernels  63.2 us (91%)
  between operations  3.73 us (5%)
  local copies, waits for them, and re-layouts  1.92 us (3%)
    pallas_call x1, Pallas kernels, body(): pl.pallas_call(kernel, out_shape=(jax.ShapeDtypeStruct((ROWS, D), BF16),...  63.2 us
    unnamed x1, local copies, waits for them, and re-layouts  1.92 us

profile of v2, /device:TPU:1, one launch (start us, length us, event | category | flops | bytes accessed | tf_op | source)
XLA Modules:
  0.0 68.9 jit_solution(3089160928966839500)
XLA Ops:
  1.9 63.2 %shard_map.95 = (bf16[256,1152]{1,0:T(8,128)(2,1)}, f32[1]{0:T(128)}) custom-call(bf16[256,1152]{1,0:T(8,128)(2,1)} %bitcast.6, s32[1]{0:T(128)S(6)} %copy.12.time_ref, f32[1]{0:T(128)S(6)} %copy.13.size_ref, bf16[32,6912]{1,0:T(8,128)(2,1)} %mod_hbm.1, bf16[1728,1152]{1,0:T(8,128)(2,1)} %bitcast.4, bf16[576,1152]{1,0:T(8,128)(2,1)} %o1_hbm.1, ...), custom_call_target="tpu_custom_call" | custom-call | flops 2800000000 | bytes 12000000 | tf_op jit(solution)/shard_map/pallas_call | solution.py:381
  65.2 1.9 %copy.14 = bf16[1,1,256,1152]{3,2,1,0:T(8,128)(2,1)} copy(bf16[1,1,256,1152]{3,2,1,0:T(8,128)(2,1)} %bitcast.7) | data formatting | bytes 1179648

commit v3 on v2

v3 whole, which is shorter than its diff:
```python
import math

import jax
import jax.numpy as jnp
from jax import lax
from jax.experimental import pallas as pl
from jax.experimental.pallas import tpu as pltpu
from jax.sharding import PartitionSpec as P

UNROLL = 7
NORM_ROWS = 128
PROJECT = 1728
MESH = pl.DeviceIdType.MESH
F32 = jnp.float32
BF16 = jnp.bfloat16

D = 1152
HEADS = 8
HEAD_DIM = 72
E = HEADS * HEAD_DIM
ROWS = 256
HALF = 128
PIECE = 16
NX = 4
NZ = 8
NS = 8
QUART = 64
WIDE = 640
SHIFT = 512
EPS = 1e-6
LOG2E = 1.4426950408889634
Q_SCALE = 3.0 / math.sqrt(HEAD_DIM) * LOG2E


def layer_norm(values):
    center = values - jnp.mean(values, axis=-1, keepdims=True)
    spread = jnp.mean(center * center, axis=-1, keepdims=True)
    return center * lax.rsqrt(spread + EPS)


def attend(raw, heads, scores, blocks, mask):
    def unit(start, scale):
        values = raw[pl.ds(pl.multiple_of(start, 8), HEAD_DIM), :]
        squares = jnp.sum(values * values, axis=0, keepdims=True)
        return values * (lax.rsqrt(squares * (1.0 / HEAD_DIM) + EPS) * scale)

    def ask(head):
        asked = unit(head * HEAD_DIM, Q_SCALE).astype(BF16)
        keys = unit(E + head * HEAD_DIM, 1.0).T.astype(BF16)
        for at in blocks:
            scores[lax.rem(head, 2), at, : at.stop - at.start] = jnp.dot(
                keys[at, :], asked[:, at], preferred_element_type=F32
            )

    def answer(head):
        values = raw[pl.ds(pl.multiple_of(2 * E + head * HEAD_DIM, 8), HEAD_DIM), :].astype(BF16)
        for at in blocks:
            weights = jnp.exp2(scores[lax.rem(head, 2), at, : at.stop - at.start])
            if mask is not None:
                weights = jnp.where(mask, weights, 0.0)
            inverse = 1.0 / jnp.sum(weights, axis=0, keepdims=True)
            mixed = jnp.dot(values[:, at], weights.astype(BF16), preferred_element_type=F32)
            heads[pl.ds(pl.multiple_of(head * HEAD_DIM, 8), HEAD_DIM), at] = mixed * inverse

    def one_head(head, _):
        ask(head + 1)
        answer(head)
        return _

    ask(0)
    lax.fori_loop(0, HEADS - 1, one_head, 0, unroll=UNROLL)
    answer(HEADS - 1)


def kernel(
    lat_hbm, time_hbm, size_hbm, mod_hbm, w1_hbm, o1_hbm, w2_hbm, o2_hbm,
    out_hbm, change_ref,
    time_ref, size_ref, lat, mod, w1, o1, w2, o2, cond, inputs, raw, scores, heads,
    following, after, anchor, mine, drift, x_in, total, z_in, carry, c_in, done, u_in, out,
    part, parts,
    local_sem, next_send, next_recv, anchor_send, anchor_recv, y_send, y_recv,
    x_send, x_recv, z_send, z_recv, c_send, c_recv, u_send, u_recv, p_send, p_recv, out_sem,
):
    me = lax.axis_index("step")
    s = lax.axis_index("seq")
    z, x = me // NX, lax.rem(me, NX)
    fh, cg = x // 2, lax.rem(x, 2)

    loads = [
        pltpu.make_async_copy(src, dst, local_sem.at[i])
        for i, (src, dst) in enumerate(
            [
                (lat_hbm, lat), (mod_hbm, mod), (w1_hbm, w1), (o1_hbm, o1), (w2_hbm, w2), (o2_hbm, o2),
                (time_hbm, time_ref), (size_hbm, size_ref),
            ]
        )
    ]
    for load in loads:
        load.start()

    def to(step, seq):
        return {"step": step, "seq": seq}

    barrier = pltpu.get_barrier_semaphore()
    before = lax.rem(me + NX * NZ - 1, NX * NZ)
    behind = lax.rem(me + 1, NX * NZ)

    def greet_plane(k, _):
        other_s = lax.rem(s + lax.rem(k, NS), NS)
        other_x = lax.rem(x + k // NS, NX)
        pl.semaphore_signal(barrier, inc=1, device_id=to(z * NX + other_x, other_s), device_id_type=MESH)
        return _

    lax.fori_loop(1, NX * NS, greet_plane, 0)

    def greet_planes(k, _):
        other_z = lax.rem(z + k, NZ)
        pl.semaphore_signal(barrier, inc=1, device_id=to(other_z * NX + x, s), device_id_type=MESH)
        return _

    lax.fori_loop(1, NZ, greet_planes, 0)
    for step in (before, behind):
        pl.semaphore_signal(barrier, inc=1, device_id=to(step, s), device_id_type=MESH)

    loads[6].wait()
    loads[7].wait()
    loads[1].wait()
    one_hot = (lax.broadcasted_iota(jnp.int32, (16, mod.shape[0]), 1) == time_ref[0]).astype(BF16)
    cond[...] = jnp.dot(one_hot, mod[...], preferred_element_type=F32)[:8]

    def vector(i):
        return cond[0:1, i * D : (i + 1) * D]

    def condition(src, shift, scale):
        def some(i, _):
            rows = pl.ds(pl.multiple_of(i * NORM_ROWS, NORM_ROWS), NORM_ROWS)
            normal = layer_norm(src[rows, :].astype(F32))
            inputs[rows, :] = (normal * (1.0 + vector(scale)) + vector(shift)).astype(BF16)
            return _

        lax.fori_loop(0, ROWS // NORM_ROWS, some, 0)

    def piece(k, half):
        return pl.ds(pl.multiple_of(half * HALF + k * PIECE, PIECE), PIECE)

    def y_start(src, dst, send, recv, half):
        def start(k, _):
            target = lax.rem(s + k, NS)
            pltpu.make_async_remote_copy(
                src_ref=src.at[piece(target, half), :], dst_ref=dst.at[piece(s, half), :],
                send_sem=send, recv_sem=recv, device_id=to(me, target), device_id_type=MESH,
            ).start()
            return _

        lax.fori_loop(1, NS, start, 0)
        dst[piece(s, half), :] = src[piece(s, half), :]

    def moved(ref, sem):
        pltpu.make_async_copy(ref, ref, sem).wait()

    loads[0].wait()
    condition(lat, 0, 1)
    pl.semaphore_wait(barrier, NX * NS - 1 + NZ - 1 + 2)

    @pl.when(me == 0)
    def _():
        for half in range(2):
            y_start(lat, anchor, anchor_send, anchor_recv, half)

    send_next = pltpu.make_async_remote_copy(
        src_ref=lat, dst_ref=following, send_sem=next_send, recv_sem=next_recv,
        device_id=to(before, s), device_id_type=MESH,
    )
    send_next.start()

    contract_last = (((1,), (1,)), ((), ()))
    contract_first = (((0,), (0,)), ((), ()))
    halves = [slice(half * HALF, (half + 1) * HALF) for half in range(2)]

    def project(weights):
        def some(i, _):
            rows = pl.ds(pl.multiple_of(i * PROJECT, 16), PROJECT)
            raw[rows, :] = lax.dot_general(
                weights[rows, :], inputs[...], contract_last, preferred_element_type=F32
            )
            return _

        lax.fori_loop(0, 3 * E // PROJECT, some, 0)

    loads[2].wait()
    project(w1)
    attend(raw, heads, scores, (slice(0, ROWS),), None)
    loads[3].wait()

    def spatial_out(half, _):
        rows = pl.ds(pl.multiple_of(half * HALF, HALF), HALF)
        shown = lax.dot_general(
            heads[:, rows].astype(BF16), o1[...], contract_first, preferred_element_type=F32
        )
        after[rows, :] = (lat[rows, :].astype(F32) + vector(2) * shown).astype(BF16)
        y_start(after, mine, y_send, y_recv.at[half], half)
        return _

    lax.fori_loop(0, 2, spatial_out, 0, unroll=2)
    loads[4].wait()
    loads[5].wait()

    def block(half, holder):
        row = pl.multiple_of(half * HALF + (holder // 2) * QUART, QUART)
        col = pl.multiple_of(lax.rem(holder, 2) * SHIFT, 128)
        return pl.ds(row, QUART), pl.ds(col, WIDE)

    def x_start(half):
        for k in range(1, NX):
            target = lax.rem(x + k, NX)
            pltpu.make_async_remote_copy(
                src_ref=drift.at[block(half, target)], dst_ref=x_in.at[half, x],
                send_sem=x_send, recv_sem=x_recv.at[half],
                device_id=to(z * NX + target, s), device_id_type=MESH,
            ).start()
        x_in[half, x] = drift[block(half, x)]

    for half in range(2):
        moved(mine.at[pl.ds(half * HALF, HALF - PIECE), :], y_recv.at[half])
    condition(mine, 3, 4)
    project(w2)
    patch = lax.rem(lax.broadcasted_iota(jnp.int32, (HALF, HALF), 0), PIECE)
    patch_of_key = lax.rem(lax.broadcasted_iota(jnp.int32, (HALF, HALF), 1), PIECE)
    attend(raw, heads, scores, halves, patch == patch_of_key)

    @pl.when(me == 0)
    def _():
        moved(anchor.at[pl.ds(0, ROWS - 2 * PIECE), :], anchor_recv)

    def temporal_out(half, held):
        rows = pl.ds(pl.multiple_of(half * HALF, HALF), HALF)
        shown = lax.dot_general(
            heads[:, rows].astype(BF16), o2[...], contract_first, preferred_element_type=F32
        )
        drift[rows, :] = (size_ref[0] * (mine[rows, :].astype(F32) + vector(5) * shown)).astype(BF16)

        @pl.when(me == 0)
        def _():
            drift[rows, :] = (drift[rows, :].astype(F32) + anchor[rows, :].astype(F32)).astype(BF16)

        x_start(half)
        return held

    lax.fori_loop(0, 2, temporal_out, 0, unroll=2)

    for half in range(2):
        moved(x_in.at[half, pl.ds(0, NX - 1)], x_recv.at[half])
        block_sum = x_in[half, 0].astype(F32)
        for k in range(1, NX):
            block_sum = block_sum + x_in[half, k].astype(F32)
        total[half] = block_sum.astype(BF16).reshape(4, PIECE, WIDE)
        for frame in range(4):
            target = 2 * frame + half

            @pl.when(z != target)
            def _():
                pltpu.make_async_remote_copy(
                    src_ref=total.at[half, frame], dst_ref=z_in.at[z],
                    send_sem=z_send, recv_sem=z_recv,
                    device_id=to(target * NX + x, s), device_id_type=MESH,
                ).start()

            @pl.when(z == target)
            def _():
                z_in[z] = total[half, frame]

    for half in range(2):

        @pl.when(lax.rem(z, 2) == half)
        def _():
            moved(z_in.at[pl.ds(0, NZ - 1)], z_recv)
            running = jnp.zeros((PIECE, WIDE), F32)
            for k in range(NZ):
                carry[k] = running.astype(BF16)
                running = running + z_in[k].astype(F32)
            for k in range(1, NZ):
                target = lax.rem(z + k, NZ)
                pltpu.make_async_remote_copy(
                    src_ref=carry.at[target], dst_ref=c_in.at[half, z // 2],
                    send_sem=c_send, recv_sem=c_recv.at[half],
                    device_id=to(target * NX + x, s), device_id_type=MESH,
                ).start()
            c_in[half, z // 2] = carry[z]

    for half in range(2):

        @pl.when(lax.rem(z, 2) == half)
        def _():
            moved(c_in.at[half, pl.ds(0, 3)], c_recv.at[half])

        @pl.when(lax.rem(z, 2) != half)
        def _():
            moved(c_in.at[half], c_recv.at[half])

        running = c_in[half].astype(F32).reshape(QUART, WIDE)
        for k in range(NX):
            running = running + x_in[half, k].astype(F32)
            done[half, k] = running.astype(BF16).reshape(4, PIECE, WIDE)

        def u_start(k, held):
            x_to, frame = lax.rem(x + k // 4, NX), lax.rem(k, 4)

            @pl.when(jnp.logical_or(x_to != x, fh * 4 + frame != s))
            def _():
                pltpu.make_async_remote_copy(
                    src_ref=done.at[half, x_to, frame], dst_ref=u_in.at[cg, piece(s, half), :],
                    send_sem=u_send, recv_sem=u_recv.at[half],
                    device_id=to(z * NX + x_to, fh * 4 + frame), device_id_type=MESH,
                ).start()

            return held

        lax.fori_loop(0, NX * 4, u_start, 0)

        @pl.when(s // 4 == fh)
        def _():
            u_in[cg, piece(s, half), :] = done[half, x, lax.rem(s, 4)]

    send_next.wait_recv()
    known = jnp.where(me == NX * NZ - 1, 0.0, 1.0)
    part[...] = jnp.zeros_like(part)
    stores = []
    for half in range(2):
        rows = halves[half]

        @pl.when(s // 4 == fh)
        def _():
            moved(u_in.at[0, pl.ds(0, ROWS - PIECE), :], u_recv.at[half])

        @pl.when(s // 4 != fh)
        def _():
            moved(u_in.at[0], u_recv.at[half])

        out[rows, :WIDE] = u_in[0, rows, :]
        out[rows, WIDE:] = u_in[1, rows, 128:]
        store = pltpu.make_async_copy(out.at[rows, :], out_hbm.at[rows, :], out_sem.at[half])
        store.start()
        stores.append(store)
        goal = jnp.where(known > 0.5, following[rows, :].astype(F32), 0.0)
        difference = out[rows, :].astype(F32) - goal
        squares = (difference * difference).reshape(HALF // 8, 8, D).sum(axis=0)
        for t in range(D // 128):
            part[...] += squares[:, t * 128 : (t + 1) * 128]

    for k in range(1, NS):
        pltpu.make_async_remote_copy(
            src_ref=part, dst_ref=parts.at[s], send_sem=p_send, recv_sem=p_recv,
            device_id=to(me, lax.rem(s + k, NS)), device_id_type=MESH,
        ).start()
    parts[s] = part[...]
    moved(parts.at[pl.ds(0, NS - 1)], p_recv)
    change_ref[0] = jnp.sum(jnp.sum(parts[...], axis=0)) * (1.0 / (NS * ROWS * D))

    send_next.wait_send()

    @pl.when(me == 0)
    def _():
        moved(anchor.at[pl.ds(0, ROWS - 2 * PIECE), :], anchor_send)

    moved(mine.at[pl.ds(0, ROWS - 2 * PIECE), :], y_send)
    moved(x_in.at[:, pl.ds(0, NX - 1)], x_send)
    moved(z_in.at[pl.ds(0, NZ - 1)], z_send)
    moved(carry.at[pl.ds(0, NZ - 1)], c_send)

    @pl.when(s // 4 == fh)
    def _():
        moved(u_in.at[:, pl.ds(0, ROWS - PIECE), :], u_send)

    @pl.when(s // 4 != fh)
    def _():
        moved(u_in, u_send)

    moved(parts.at[pl.ds(0, NS - 1)], p_send)
    for store in stores:
        store.wait()


def body(latents, timesteps, step_sizes, modulation, spatial_qkv, spatial_out, temporal_qkv, temporal_out):
    dma = pltpu.SemaphoreType.DMA

    def vmem(*shape, dtype=BF16):
        return pltpu.VMEM(shape, dtype)

    table = modulation.shape[0]
    updated, change = pl.pallas_call(
        kernel,
        out_shape=(jax.ShapeDtypeStruct((ROWS, D), BF16), jax.ShapeDtypeStruct((1,), F32)),
        in_specs=[pl.BlockSpec(memory_space=pltpu.HBM)] * 8,
        out_specs=(pl.BlockSpec(memory_space=pl.ANY), pl.BlockSpec(memory_space=pltpu.SMEM)),
        scratch_shapes=[
            pltpu.SMEM((1,), jnp.int32), pltpu.SMEM((1,), F32),
            vmem(ROWS, D), vmem(table, 6 * D),
            vmem(3 * E, D), vmem(E, D), vmem(3 * E, D), vmem(E, D),
            vmem(8, 6 * D, dtype=F32), vmem(ROWS, D),
            vmem(3 * E, ROWS, dtype=F32), vmem(2, ROWS, ROWS, dtype=F32), vmem(E, ROWS, dtype=F32),
            vmem(ROWS, D), vmem(ROWS, D), vmem(ROWS, D), vmem(ROWS, D), vmem(ROWS, D),
            vmem(2, NX, QUART, WIDE), vmem(2, 4, PIECE, WIDE), vmem(NZ, PIECE, WIDE),
            vmem(NZ, PIECE, WIDE), vmem(2, 4, PIECE, WIDE),
            vmem(2, NX, 4, PIECE, WIDE), vmem(2, ROWS, WIDE), vmem(ROWS, D),
            vmem(8, 128, dtype=F32), vmem(NS, 8, 128, dtype=F32),
            dma((8,)), dma, dma, dma, dma, dma, dma((2,)),
            dma, dma((2,)), dma, dma, dma, dma((2,)), dma, dma((2,)), dma, dma, dma((2,)),
        ],
        compiler_params=pltpu.CompilerParams(
            collective_id=0, has_side_effects=True, vmem_limit_bytes=40 * 1024 * 1024
        ),
        cost_estimate=pl.CostEstimate(
            flops=2800000000, bytes_accessed=12000000, transcendentals=1000000
        ),
    )(
        latents.reshape(ROWS, D), timesteps, step_sizes, modulation,
        spatial_qkv.T, spatial_out, temporal_qkv.T, temporal_out,
    )
    return updated[None, None], change


def solution(mesh):
    in_specs = (P("step", "seq", None, None), P("step"), P("step"), P(), P(), P(), P(), P())
    out_specs = (P("step", "seq", None, None), P("step"))
    return jax.shard_map(body, mesh=mesh, in_specs=in_specs, out_specs=out_specs, check_vma=False)
```

time: 69.1 us -> 77 us (1.11)
  local copies, waits for them, and re-layouts: 1.92 us -> 9.78 us
    unnamed x1 -> x13, local copies, waits for them, and re-layouts: 1.92 us -> 9.78 us
where the time goes in v3:
time: 77 us; the launch traced here: 76.6 us
  Pallas kernels  63.1 us (82%)
  local copies, waits for them, and re-layouts  9.78 us (13%)
  between operations  3.76 us (5%)
    pallas_call x1, Pallas kernels, body(): pl.pallas_call(kernel, out_shape=(jax.ShapeDtypeStruct((ROWS, D), BF16),...  63.1 us
    unnamed x13, local copies, waits for them, and re-layouts  9.78 us

profile of v3, /device:TPU:1, one launch (start us, length us, event | category | flops | bytes accessed | tf_op | source)
XLA Modules:
  0.0 76.6 jit_solution(2667384064591532049)
XLA Ops:
  1.9 0.0 copy-start
  1.9 2.1 %copy-done = bf16[1152,1728]{0,1:T(8,128)(2,1)S(1)} copy-done((bf16[1152,1728]{0,1:T(8,128)(2,1)S(1)}, bf16[1152,1728]{0,1:T(8,128)(2,1)}, u32[]{:S(2)}) %copy-start) | copy-done | bytes 3981336
  4.0 0.0 copy-start.1
  4.1 2.1 %copy-done.1 = bf16[1152,1728]{0,1:T(8,128)(2,1)S(1)} copy-done((bf16[1152,1728]{0,1:T(8,128)(2,1)S(1)}, bf16[1152,1728]{0,1:T(8,128)(2,1)}, u32[]{:S(2)}) %copy-start.1) | copy-done | bytes 3981336
  6.2 0.0 copy-start.2
  6.2 1.3 %copy-done.2 = bf16[576,1152]{1,0:T(8,128)(2,1)S(1)} copy-done((bf16[576,1152]{1,0:T(8,128)(2,1)S(1)}, bf16[576,1152]{1,0:T(8,128)(2,1)}, u32[]{:S(2)}) %copy-start.2) | copy-done | bytes 1327128
  7.5 0.0 copy-start.3
  7.5 1.3 %copy-done.3 = bf16[576,1152]{1,0:T(8,128)(2,1)S(1)} copy-done((bf16[576,1152]{1,0:T(8,128)(2,1)S(1)}, bf16[576,1152]{1,0:T(8,128)(2,1)}, u32[]{:S(2)}) %copy-start.3) | copy-done | bytes 1327128
  8.8 0.0 copy-start.4
  8.8 1.1 %copy-done.4 = bf16[1,1,256,1152]{3,2,1,0:T(8,128)(2,1)S(1)} copy-done((bf16[1,1,256,1152]{3,2,1,0:T(8,128)(2,1)S(1)}, bf16[1,1,256,1152]{3,2,1,0:T(8,128)(2,1)}, u32[]{:S(2)}) %copy-start.4) | copy-done | bytes 589848
  9.9 0.0 copy-start.5
  9.9 1.0 %copy-done.5 = bf16[32,6912]{1,0:T(8,128)(2,1)S(1)} copy-done((bf16[32,6912]{1,0:T(8,128)(2,1)S(1)}, bf16[32,6912]{1,0:T(8,128)(2,1)}, u32[]{:S(2)}) %copy-start.5) | copy-done | bytes 442392
  10.9 63.1 %shard_map.95 = (bf16[256,1152]{1,0:T(8,128)(2,1)S(1)}, f32[1]{0:T(128)}) custom-call(bf16[256,1152]{1,0:T(8,128)(2,1)S(1)} %bitcast.6, s32[1]{0:T(128)S(6)} %copy.12.time_hbm, f32[1]{0:T(128)S(6)} %copy.13.size_hbm, bf16[32,6912]{1,0:T(8,128)(2,1)S(1)} %copy-done.5, bf16[1728,1152]{1,0:T(8,128)(2,1)S(1)} %bitcast.4, bf16[576,1152]{1,0:T(8,128)(2,1)S(1)} %copy-done.2, ...), custom_call_target="tpu_custom_call" | custom-call | flops 2800000000 | bytes 12000000 | tf_op jit(solution)/shard_map/pallas_call | solution.py:390
  74.0 0.8 %copy.14 = bf16[1,1,256,1152]{3,2,1,0:T(8,128)(2,1)} copy(bf16[1,1,256,1152]{3,2,1,0:T(8,128)(2,1)S(1)} %bitcast.7) | data formatting | bytes 1179648
Async XLA Ops:
  1.9 2.1 %copy-start = (bf16[1152,1728]{0,1:T(8,128)(2,1)S(1)}, bf16[1152,1728]{0,1:T(8,128)(2,1)}, u32[]{:S(2)}) copy-start(bf16[1152,1728]{0,1:T(8,128)(2,1)} %param.12) | copy-start | bytes 11943940
  4.0 2.1 %copy-start.1 = (bf16[1152,1728]{0,1:T(8,128)(2,1)S(1)}, bf16[1152,1728]{0,1:T(8,128)(2,1)}, u32[]{:S(2)}) copy-start(bf16[1152,1728]{0,1:T(8,128)(2,1)} %param.14) | copy-start | bytes 11943940
  6.2 1.3 %copy-start.2 = (bf16[576,1152]{1,0:T(8,128)(2,1)S(1)}, bf16[576,1152]{1,0:T(8,128)(2,1)}, u32[]{:S(2)}) copy-start(bf16[576,1152]{1,0:T(8,128)(2,1)} %o1_hbm.1) | copy-start | bytes 3981316
  7.5 1.3 %copy-start.3 = (bf16[576,1152]{1,0:T(8,128)(2,1)S(1)}, bf16[576,1152]{1,0:T(8,128)(2,1)}, u32[]{:S(2)}) copy-start(bf16[576,1152]{1,0:T(8,128)(2,1)} %o2_hbm.1) | copy-start | bytes 3981316
  8.8 1.1 %copy-start.4 = (bf16[1,1,256,1152]{3,2,1,0:T(8,128)(2,1)S(1)}, bf16[1,1,256,1152]{3,2,1,0:T(8,128)(2,1)}, u32[]{:S(2)}) copy-start(bf16[1,1,256,1152]{3,2,1,0:T(8,128)(2,1)} %param.8) | copy-start | bytes 1769476
  9.9 1.0 %copy-start.5 = (bf16[32,6912]{1,0:T(8,128)(2,1)S(1)}, bf16[32,6912]{1,0:T(8,128)(2,1)}, u32[]{:S(2)}) copy-start(bf16[32,6912]{1,0:T(8,128)(2,1)} %mod_hbm.1) | copy-start | bytes 1327108

commit v4 on v3

v4 whole, which is shorter than its diff:
```python
import math

import jax
import jax.numpy as jnp
from jax import lax
from jax.experimental import pallas as pl
from jax.experimental.pallas import tpu as pltpu
from jax.sharding import PartitionSpec as P

UNROLL = 7
PROJECT = 864
MESH = pl.DeviceIdType.MESH
F32 = jnp.float32
BF16 = jnp.bfloat16

D = 1152
HEADS = 8
HEAD_DIM = 72
E = HEADS * HEAD_DIM
ROWS = 256
HALF = 128
PIECE = 8
NX = 4
NZ = 8
NS = 8
STEP_ROWS = NS * PIECE
EPS = 1e-6
LOG2E = 1.4426950408889634
Q_SCALE = 3.0 / math.sqrt(HEAD_DIM) * LOG2E


def layer_norm(values):
    center = values - jnp.mean(values, axis=-1, keepdims=True)
    spread = jnp.mean(center * center, axis=-1, keepdims=True)
    return center * lax.rsqrt(spread + EPS)


def attend(raw, heads, scores, blocks, mask):
    def unit(start, scale):
        values = raw[pl.ds(pl.multiple_of(start, 8), HEAD_DIM), :]
        squares = jnp.sum(values * values, axis=0, keepdims=True)
        return values * (lax.rsqrt(squares * (1.0 / HEAD_DIM) + EPS) * scale)

    def ask(head):
        asked = unit(head * HEAD_DIM, Q_SCALE).astype(BF16)
        keys = unit(E + head * HEAD_DIM, 1.0).T.astype(BF16)
        for at in blocks:
            scores[lax.rem(head, 2), at, : at.stop - at.start] = jnp.dot(
                keys[at, :], asked[:, at], preferred_element_type=F32
            )

    def answer(head):
        values = raw[pl.ds(pl.multiple_of(2 * E + head * HEAD_DIM, 8), HEAD_DIM), :].astype(BF16)
        for at in blocks:
            weights = jnp.exp2(scores[lax.rem(head, 2), at, : at.stop - at.start])
            if mask is not None:
                weights = jnp.where(mask, weights, 0.0)
            inverse = 1.0 / jnp.sum(weights, axis=0, keepdims=True)
            mixed = jnp.dot(values[:, at], weights.astype(BF16), preferred_element_type=F32)
            heads[pl.ds(pl.multiple_of(head * HEAD_DIM, 8), HEAD_DIM), at] = mixed * inverse

    def one_head(head, _):
        ask(head + 1)
        answer(head)
        return _

    ask(0)
    lax.fori_loop(0, HEADS - 1, one_head, 0, unroll=UNROLL)
    answer(HEADS - 1)


def kernel(
    lat_hbm, time_hbm, size_hbm, mod_hbm, w1_hbm, o1_hbm, w2_hbm, o2_hbm,
    out, change_ref,
    time_ref, size_ref, lat, mod, w1, o1, w2, o2, cond, inputs, raw, scores, heads,
    after, mine, temper, following, drift, total, z_in, carry, c_in, done, part, parts,
    local_sem, temper_send, temper_recv, y_send, y_recv, next_send, next_recv,
    z_send, z_recv, c_send, c_recv, u_send, u_recv, p_send, p_recv, own_sem,
):
    me = lax.axis_index("step")
    s = lax.axis_index("seq")
    z, x = me // NX, lax.rem(me, NX)

    loads = [
        pltpu.make_async_copy(src, dst, local_sem.at[i])
        for i, (src, dst) in enumerate(
            [
                (mod_hbm, mod), (lat_hbm, lat), (w1_hbm, w1), (o1_hbm, o1), (w2_hbm, w2), (o2_hbm, o2),
                (time_hbm, time_ref), (size_hbm, size_ref),
            ]
        )
    ]
    for i in (6, 7, 0, 1, 2, 3, 4, 5):
        loads[i].start()

    def to(step, seq):
        return {"step": step, "seq": seq}

    def greet(step, seq):
        pl.semaphore_signal(barrier, inc=1, device_id=to(step, seq), device_id_type=MESH)

    barrier = pltpu.get_barrier_semaphore()

    def greet_plane(k, _):
        greet(z * NX + lax.rem(x + k // NS, NX), lax.rem(s + lax.rem(k, NS), NS))
        return _

    lax.fori_loop(1, NX * NS, greet_plane, 0)

    def greet_planes(k, _):
        greet(lax.rem(z + k, NZ) * NX + x, s)
        return _

    lax.fori_loop(1, NZ, greet_planes, 0)

    @pl.when(z < NZ - 1)
    def _():
        def greet_next(k, held):
            greet((z + 1) * NX, lax.rem(s + k, NS))
            return held

        lax.fori_loop(0, NS, greet_next, 0)

    loads[6].wait()
    loads[7].wait()
    loads[0].wait()
    one_hot = (lax.broadcasted_iota(jnp.int32, (16, mod.shape[0]), 1) == time_ref[0]).astype(BF16)
    cond[...] = jnp.dot(one_hot, mod[...], preferred_element_type=F32)[:8]

    def vector(i):
        return cond[0:1, i * D : (i + 1) * D]

    temper[x] = jnp.concatenate(
        [vector(3), 1.0 + vector(4), vector(5) * size_ref[0], jnp.broadcast_to(size_ref[0], (5, D))], axis=0
    )

    def moved(ref, sem):
        pltpu.make_async_copy(ref, ref, sem).wait()

    def normal_in(src, i, shift, scale, pieces):
        rows = pl.ds(pl.multiple_of(i * pieces * PIECE, pieces * PIECE), pieces * PIECE)
        values = src[pl.ds(i * pieces, pieces)].astype(F32).reshape(pieces * PIECE, D)
        inputs[rows, :] = (layer_norm(values) * scale + shift).astype(BF16)

    loads[1].wait()

    def spatial_in(i, _):
        normal_in(lat, i, vector(0), 1.0 + vector(1), 16)
        return _

    lax.fori_loop(0, 2, spatial_in, 0)

    contract_last = (((1,), (1,)), ((), ()))
    contract_first = (((0,), (0,)), ((), ()))

    def project(weights):
        def some(i, _):
            rows = pl.ds(pl.multiple_of(i * PROJECT, 16), PROJECT)
            raw[rows, :] = lax.dot_general(
                weights[rows, :], inputs[...], contract_last, preferred_element_type=F32
            )
            return _

        lax.fori_loop(0, 3 * E // PROJECT, some, 0)

    loads[2].wait()
    project(w1)
    attend(raw, heads, scores, (slice(0, ROWS),), None)
    loads[3].wait()

    @pl.when(jnp.logical_and(x == 0, z > 0))
    def _():
        pl.semaphore_wait(barrier, 2 * NX * NS - 1 + NZ - 1)

    @pl.when(jnp.logical_not(jnp.logical_and(x == 0, z > 0)))
    def _():
        pl.semaphore_wait(barrier, NX * NS - 1 + NZ - 1)

    def place(x_at, s_at):
        return lax.rem(s_at, 2) * 16 + (s_at // 2) * 4 + x_at

    own = place(x, s)

    for k in range(1, NX):
        pltpu.make_async_remote_copy(
            src_ref=temper.at[x], dst_ref=temper.at[x], send_sem=temper_send, recv_sem=temper_recv,
            device_id=to(z * NX + lax.rem(x + k, NX), s), device_id_type=MESH,
        ).start()

    for half in range(2):
        rows = slice(half * HALF, (half + 1) * HALF)
        pieces = slice(half * 16, (half + 1) * 16)
        shown = lax.dot_general(
            heads[:, rows].astype(BF16), o1[...], contract_first, preferred_element_type=F32
        )
        state = lat[pieces].astype(F32).reshape(HALF, D)
        after[pieces] = (state + vector(2) * shown).reshape(16, PIECE, D).astype(BF16)

        def y_start(k, _):
            x_to = lax.rem(x + k // 4, NX)
            s_to = lax.rem(s // 2 + lax.rem(k, 4), 4) * 2 + half

            @pl.when(jnp.logical_or(x_to != x, s_to != s))
            def _():
                pltpu.make_async_remote_copy(
                    src_ref=after.at[place(x_to, s_to)], dst_ref=mine.at[x * NS + s],
                    send_sem=y_send, recv_sem=y_recv,
                    device_id=to(z * NX + x_to, s_to), device_id_type=MESH,
                ).start()

            return k

        lax.fori_loop(0, 16, y_start, 0)
    mine[x * NS + s] = after[own]

    first = me == 0
    plane = jnp.where(jnp.logical_and(x == 0, z > 0), z - 1, z)
    slot = jnp.where(first, NX, lax.rem(x + NX - 1, NX))
    kind = jnp.where(first, 2, jnp.where(x == 0, 1, 0))

    def next_start(k, _):
        x_to, s_to = lax.rem(x + k // NS, NX), lax.rem(s + lax.rem(k, NS), NS)
        pltpu.make_async_remote_copy(
            src_ref=lat.at[place(x_to, s_to)], dst_ref=following.at[slot, s],
            send_sem=next_send, recv_sem=next_recv.at[kind],
            device_id=to(plane * NX + x_to, s_to), device_id_type=MESH,
        ).start()
        return _

    lax.fori_loop(1, NX * NS, next_start, 0)

    @pl.when(plane != z)
    def _():
        next_start(0, 0)

    @pl.when(plane == z)
    def _():
        following[slot, s] = lat[own]

    @pl.when(z == NZ - 1)
    def _():
        following[NX - 1] = jnp.zeros(following.shape[1:], BF16)

    loads[4].wait()
    loads[5].wait()
    moved(temper.at[pl.ds(0, NX - 1)], temper_recv)
    moved(mine.at[pl.ds(0, NX * NS - 1)], y_recv)

    def temporal_in(i, _):
        normal_in(mine, i, temper[i, 0:1, :], temper[i, 1:2, :], NS)
        return _

    lax.fori_loop(0, NX, temporal_in, 0, unroll=2)
    project(w2)
    row = lax.broadcasted_iota(jnp.int32, (HALF, HALF), 0)
    col = lax.broadcasted_iota(jnp.int32, (HALF, HALF), 1)
    same = jnp.logical_and(row // STEP_ROWS == col // STEP_ROWS, lax.rem(row, PIECE) == lax.rem(col, PIECE))
    attend(raw, heads, scores, (slice(0, HALF), slice(HALF, ROWS)), same)
    for half in range(2):
        rows = slice(half * HALF, (half + 1) * HALF)
        shown = lax.dot_general(
            heads[:, rows].astype(BF16), o2[...], contract_first, preferred_element_type=F32
        )
        for i in range(2):
            step = half * 2 + i
            state = mine[step * NS : (step + 1) * NS].astype(F32).reshape(STEP_ROWS, D)
            drift[step] = (
                state * temper[step, 3:4, :]
                + temper[step, 2:3, :] * shown[i * STEP_ROWS : (i + 1) * STEP_ROWS]
            )

    @pl.when(z == 0)
    def _():
        @pl.when(first)
        def _():
            moved(following.at[NX, pl.ds(0, NS - 1)], next_recv.at[2])

        @pl.when(jnp.logical_not(first))
        def _():
            moved(following.at[NX], next_recv.at[2])

        drift[0] = drift[0] + following[NX].astype(F32).reshape(STEP_ROWS, D)

    everything = drift[0] + drift[1] + drift[2] + drift[3]
    total[...] = everything.reshape(NS, PIECE, D).astype(BF16)

    def z_start(k, _):
        target = lax.rem(z + k, NZ)
        pltpu.make_async_remote_copy(
            src_ref=total.at[target], dst_ref=z_in.at[z], send_sem=z_send, recv_sem=z_recv,
            device_id=to(target * NX + x, s), device_id_type=MESH,
        ).start()
        return _

    lax.fori_loop(1, NZ, z_start, 0)
    z_in[z] = total[z]
    moved(z_in.at[pl.ds(0, NZ - 1)], z_recv)
    running = jnp.zeros((PIECE, D), F32)
    for k in range(NZ):
        carry[k] = running.astype(BF16)
        running = running + z_in[k].astype(F32)

    def c_start(k, held):
        target = lax.rem(z + k, NZ)

        @pl.when(target > 0)
        def _():
            pltpu.make_async_remote_copy(
                src_ref=carry.at[target], dst_ref=c_in.at[z], send_sem=c_send, recv_sem=c_recv,
                device_id=to(target * NX + x, s), device_id_type=MESH,
            ).start()

        return held

    lax.fori_loop(1, NZ, c_start, 0)

    @pl.when(z == 0)
    def _():
        c_in[...] = jnp.zeros(c_in.shape, BF16)

    @pl.when(z > 0)
    def _():
        c_in[z] = carry[z]
        moved(c_in.at[pl.ds(0, NZ - 1)], c_recv)

    running = c_in[...].astype(F32).reshape(STEP_ROWS, D)
    for step in range(NX):
        running = running + drift[step]
        done[step] = running.reshape(NS, PIECE, D).astype(BF16)

    def u_start(k, _):
        x_to, s_to = lax.rem(x + k // NS, NX), lax.rem(s + lax.rem(k, NS), NS)
        pltpu.make_async_remote_copy(
            src_ref=done.at[x_to, s_to], dst_ref=out.at[own], send_sem=u_send, recv_sem=u_recv,
            device_id=to(z * NX + x_to, s_to), device_id_type=MESH,
        ).start()
        return _

    lax.fori_loop(1, NX * NS, u_start, 0)
    keep = pltpu.make_async_copy(done.at[x, s], out.at[own], own_sem)
    keep.start()

    @pl.when(x == 0)
    def _():
        moved(following.at[pl.ds(0, NX - 1)], next_recv.at[0])

    @pl.when(x > 0)
    def _():
        moved(mine.at[pl.ds(0, (NX - 1) * NS - 1)], next_recv.at[0])

    @pl.when(z < NZ - 1)
    def _():
        moved(following.at[0], next_recv.at[1])

    for step in range(NX):
        difference = done[step].astype(F32) - following[step].astype(F32)
        squares = jnp.sum(difference * difference, axis=0)
        tile = squares[:, :128]
        for t in range(1, D // 128):
            tile = tile + squares[:, t * 128 : (t + 1) * 128]
        part[step] = tile

    def p_start(k, _):
        x_to, s_to = lax.rem(x + k // NS, NX), lax.rem(s + lax.rem(k, NS), NS)
        pltpu.make_async_remote_copy(
            src_ref=part.at[x_to], dst_ref=parts.at[x * NS + s], send_sem=p_send, recv_sem=p_recv,
            device_id=to(z * NX + x_to, s_to), device_id_type=MESH,
        ).start()
        return _

    lax.fori_loop(1, NX * NS, p_start, 0)
    parts[x * NS + s] = part[x]

    moved(temper.at[pl.ds(0, NX - 1)], temper_send)
    moved(mine.at[pl.ds(0, NX * NS - 1)], y_send)

    @pl.when(plane != z)
    def _():
        moved(mine, next_send)

    @pl.when(plane == z)
    def _():
        moved(mine.at[pl.ds(0, NX * NS - 1)], next_send)

    moved(z_in.at[pl.ds(0, NZ - 1)], z_send)

    @pl.when(z == 0)
    def _():
        moved(carry.at[pl.ds(0, NZ - 1)], c_send)

    @pl.when(z > 0)
    def _():
        moved(carry.at[pl.ds(0, NZ - 2)], c_send)

    keep.wait()
    moved(mine.at[pl.ds(0, NX * NS - 1)], u_send)
    moved(parts.at[pl.ds(0, NX * NS - 1)], p_send)
    moved(mine.at[pl.ds(0, NX * NS - 1)], u_recv)
    moved(parts.at[pl.ds(0, NX * NS - 1)], p_recv)
    change_ref[0] = jnp.sum(jnp.sum(parts[...], axis=0)) * (1.0 / (NS * ROWS * D))


def body(latents, timesteps, step_sizes, modulation, spatial_qkv, spatial_out, temporal_qkv, temporal_out):
    dma = pltpu.SemaphoreType.DMA

    def vmem(*shape, dtype=BF16):
        return pltpu.VMEM(shape, dtype)

    def pieces(*count):
        return pltpu.VMEM((count or (NX * NS,)) + (PIECE, D), BF16)

    table = modulation.shape[0]
    updated, change = pl.pallas_call(
        kernel,
        out_shape=(jax.ShapeDtypeStruct((NX * NS, PIECE, D), BF16), jax.ShapeDtypeStruct((1,), F32)),
        in_specs=[pl.BlockSpec(memory_space=pl.ANY)] * 8,
        out_specs=(pl.BlockSpec(memory_space=pl.ANY), pl.BlockSpec(memory_space=pltpu.SMEM)),
        scratch_shapes=[
            pltpu.SMEM((1,), jnp.int32), pltpu.SMEM((1,), F32),
            pieces(), vmem(table, 6 * D),
            vmem(3 * E, D), vmem(E, D), vmem(3 * E, D), vmem(E, D),
            vmem(8, 6 * D, dtype=F32), vmem(ROWS, D),
            vmem(3 * E, ROWS, dtype=F32), vmem(2, ROWS, ROWS, dtype=F32), vmem(E, ROWS, dtype=F32),
            pieces(), pieces(), vmem(NX, 8, D, dtype=F32), pieces(NX + 1, NS),
            vmem(NX, STEP_ROWS, D, dtype=F32),
            pieces(NZ), pieces(NZ), pieces(NZ), pieces(NZ), pieces(NX, NS),
            vmem(NX, 8, 128, dtype=F32), vmem(NX * NS, 8, 128, dtype=F32),
            dma((8,)), dma, dma, dma, dma, dma, dma((3,)),
            dma, dma, dma, dma, dma, dma, dma, dma, dma,
        ],
        compiler_params=pltpu.CompilerParams(
            collective_id=0, has_side_effects=True, vmem_limit_bytes=56 * 1024 * 1024
        ),
        cost_estimate=pl.CostEstimate(
            flops=2800000000, bytes_accessed=12000000, transcendentals=1000000
        ),
    )(
        latents.reshape(NX * NS, PIECE, D), timesteps, step_sizes, modulation,
        spatial_qkv.T, spatial_out, temporal_qkv.T, temporal_out,
    )
    return updated.reshape(latents.shape), change


def solution(mesh):
    in_specs = (P("step", "seq", None, None), P("step"), P("step"), P(), P(), P(), P(), P())
    out_specs = (P("step", "seq", None, None), P("step"))
    return jax.shard_map(body, mesh=mesh, in_specs=in_specs, out_specs=out_specs, check_vma=False)
```

time: 77 us -> 59.3 us (0.77)
  the two profiles are of different devices: /device:TPU:1 before, /device:TPU:33 now
where the time goes in v4:
time: 59.3 us; the launch traced here: 59.1 us
  Pallas kernels  53.5 us (90%)
  between operations  3.73 us (6%)
  local copies, waits for them, and re-layouts  1.92 us (3%)
    pallas_call x1, Pallas kernels, body(): pl.pallas_call(kernel, out_shape=(jax.ShapeDtypeStruct((NX * NS, PIECE, D...  53.5 us
    unnamed x1, local copies, waits for them, and re-layouts  1.92 us

profile of v4, /device:TPU:33, one launch (start us, length us, event | category | flops | bytes accessed | tf_op | source)
XLA Modules:
  0.0 59.1 jit_solution(9133047346084339052)
XLA Ops:
  1.9 53.5 %shard_map.95 = (bf16[32,8,1152]{2,1,0:T(8,128)(2,1)}, f32[1]{0:T(128)}) custom-call(bf16[32,8,1152]{2,1,0:T(8,128)(2,1)} %bitcast.6, s32[1]{0:T(128)S(6)} %copy.12.time_hbm, f32[1]{0:T(128)S(6)} %copy.13.size_hbm, bf16[32,6912]{1,0:T(8,128)(2,1)} %mod_hbm.1, bf16[1728,1152]{1,0:T(8,128)(2,1)} %bitcast.4, bf16[576,1152]{1,0:T(8,128)(2,1)} %o1_hbm.1, ...), custom_call_target="tpu_custom_call" | custom-call | flops 2800000000 | bytes 12000000 | tf_op jit(solution)/shard_map/pallas_call | solution.py:413
  55.4 1.9 %copy.14 = bf16[1,1,256,1152]{3,2,1,0:T(8,128)(2,1)} copy(bf16[1,1,256,1152]{3,2,1,0:T(8,128)(2,1)} %bitcast.7) | data formatting | bytes 1179648

commit v5 on v4

--- a/solution.py
+++ b/solution.py
@@ -29,6 +29,29 @@
 Q_SCALE = 3.0 / math.sqrt(HEAD_DIM) * LOG2E
 
 
+NEAR_LAST = [
+    (2, 2), (2, 1), (2, 3), (1, 2), (3, 2), (1, 1), (3, 3), (1, 3),
+    (3, 1), (2, 0), (0, 2), (1, 0), (0, 1), (3, 0), (0, 3), (0, 0),
+]
+X_OFFSETS = sum(dx << (2 * j) for j, (dx, _) in enumerate(NEAR_LAST))
+Y_OFFSETS = sum(dy << (2 * j) for j, (_, dy) in enumerate(NEAR_LAST))
+
+
+def chip(j, x, y):
+    dx = lax.rem(lax.shift_right_logical(jnp.int32(X_OFFSETS), 2 * j), 4)
+    dy = lax.rem(lax.shift_right_logical(jnp.int32(Y_OFFSETS), 2 * j), 4)
+    return lax.rem(x + dx, 4), lax.rem(y + dy, 4)
+
+
+def other(j, x, s):
+    x_to, y_to = chip(j // 2, x, s // 2)
+    return x_to, y_to * 2 + lax.rem(s + 1 + lax.rem(j, 2), 2)
+
+
+def other_plane(j, z):
+    return lax.rem(z + NZ // 2 + (1 - 2 * lax.rem(j, 2)) * ((j + 1) // 2), NZ)
+
+
 def layer_norm(values):
     center = values - jnp.mean(values, axis=-1, keepdims=True)
     spread = jnp.mean(center * center, axis=-1, keepdims=True)
@@ -71,11 +94,11 @@
 
 def kernel(
     lat_hbm, time_hbm, size_hbm, mod_hbm, w1_hbm, o1_hbm, w2_hbm, o2_hbm,
-    out, change_ref,
+    out, parts,
     time_ref, size_ref, lat, mod, w1, o1, w2, o2, cond, inputs, raw, scores, heads,
-    after, mine, temper, following, drift, total, z_in, carry, c_in, done, part, parts,
+    after, mine, temper, following, drift, total, z_in, carry, c_in, done, part,
     local_sem, temper_send, temper_recv, y_send, y_recv, next_send, next_recv,
-    z_send, z_recv, c_send, c_recv, u_send, u_recv, p_send, p_recv, own_sem,
+    z_send, z_recv, c_send, c_recv, u_send, u_recv, p_send, p_recv, own_sem, own_part_sem,
 ):
     me = lax.axis_index("step")
     s = lax.axis_index("seq")
@@ -85,12 +108,13 @@
         pltpu.make_async_copy(src, dst, local_sem.at[i])
         for i, (src, dst) in enumerate(
             [
-                (mod_hbm, mod), (lat_hbm, lat), (w1_hbm, w1), (o1_hbm, o1), (w2_hbm, w2), (o2_hbm, o2),
+                (mod_hbm, mod), (lat_hbm, lat), (w1_hbm.at[pl.ds(0, PROJECT)], w1.at[pl.ds(0, PROJECT)]), (o1_hbm, o1), (w2_hbm, w2), (o2_hbm, o2),
                 (time_hbm, time_ref), (size_hbm, size_ref),
+                (w1_hbm.at[pl.ds(PROJECT, PROJECT)], w1.at[pl.ds(PROJECT, PROJECT)]),
             ]
         )
     ]
-    for i in (6, 7, 0, 1, 2, 3, 4, 5):
+    for i in (6, 7, 0, 1, 2, 8, 3, 4, 5):
         loads[i].start()
 
     def to(step, seq):
@@ -153,18 +177,25 @@
     contract_last = (((1,), (1,)), ((), ()))
     contract_first = (((0,), (0,)), ((), ()))
 
-    def project(weights):
-        def some(i, _):
-            rows = pl.ds(pl.multiple_of(i * PROJECT, 16), PROJECT)
-            raw[rows, :] = lax.dot_general(
-                weights[rows, :], inputs[...], contract_last, preferred_element_type=F32
-            )
-            return _
-
-        lax.fori_loop(0, 3 * E // PROJECT, some, 0)
-
-    loads[2].wait()
-    project(w1)
+    def project(weights, i):
+        rows = pl.ds(pl.multiple_of(i * PROJECT, 16), PROJECT)
+        raw[rows, :] = lax.dot_general(
+            weights[rows, :], inputs[...], contract_last, preferred_element_type=F32
+        )
+
+    def first_project(i, _):
+        @pl.when(i == 0)
+        def _():
+            loads[2].wait()
+
+        @pl.when(i == 1)
+        def _():
+            loads[8].wait()
+
+        project(w1, i)
+        return i
+
+    lax.fori_loop(0, 3 * E // PROJECT, first_project, 0)
     attend(raw, heads, scores, (slice(0, ROWS),), None)
     loads[3].wait()
 
@@ -197,8 +228,8 @@
         after[pieces] = (state + vector(2) * shown).reshape(16, PIECE, D).astype(BF16)
 
         def y_start(k, _):
-            x_to = lax.rem(x + k // 4, NX)
-            s_to = lax.rem(s // 2 + lax.rem(k, 4), 4) * 2 + half
+            x_to, y_to = chip(k, x, s // 2)
+            s_to = y_to * 2 + half
 
             @pl.when(jnp.logical_or(x_to != x, s_to != s))
             def _():
@@ -219,7 +250,7 @@
     kind = jnp.where(first, 2, jnp.where(x == 0, 1, 0))
 
     def next_start(k, _):
-        x_to, s_to = lax.rem(x + k // NS, NX), lax.rem(s + lax.rem(k, NS), NS)
+        x_to, s_to = other(k, x, s)
         pltpu.make_async_remote_copy(
             src_ref=lat.at[place(x_to, s_to)], dst_ref=following.at[slot, s],
             send_sem=next_send, recv_sem=next_recv.at[kind],
@@ -227,15 +258,18 @@
         ).start()
         return _
 
-    lax.fori_loop(1, NX * NS, next_start, 0)
-
-    @pl.when(plane != z)
-    def _():
-        next_start(0, 0)
-
-    @pl.when(plane == z)
-    def _():
-        following[slot, s] = lat[own]
+    def next_all():
+        lax.fori_loop(0, NX * NS - 1, next_start, 0)
+
+        @pl.when(plane != z)
+        def _():
+            next_start(NX * NS - 1, 0)
+
+        @pl.when(plane == z)
+        def _():
+            following[slot, s] = lat[own]
+
+    pl.when(first)(next_all)
 
     @pl.when(z == NZ - 1)
     def _():
@@ -251,7 +285,12 @@
         return _
 
     lax.fori_loop(0, NX, temporal_in, 0, unroll=2)
-    project(w2)
+
+    def second_project(i, _):
+        project(w2, i)
+        return _
+
+    lax.fori_loop(0, 3 * E // PROJECT, second_project, 0)
     row = lax.broadcasted_iota(jnp.int32, (HALF, HALF), 0)
     col = lax.broadcasted_iota(jnp.int32, (HALF, HALF), 1)
     same = jnp.logical_and(row // STEP_ROWS == col // STEP_ROWS, lax.rem(row, PIECE) == lax.rem(col, PIECE))
@@ -285,15 +324,16 @@
     total[...] = everything.reshape(NS, PIECE, D).astype(BF16)
 
     def z_start(k, _):
-        target = lax.rem(z + k, NZ)
+        target = other_plane(k, z)
         pltpu.make_async_remote_copy(
             src_ref=total.at[target], dst_ref=z_in.at[z], send_sem=z_send, recv_sem=z_recv,
             device_id=to(target * NX + x, s), device_id_type=MESH,
         ).start()
         return _
 
-    lax.fori_loop(1, NZ, z_start, 0)
+    lax.fori_loop(0, NZ - 1, z_start, 0)
     z_in[z] = total[z]
+    pl.when(jnp.logical_not(first))(next_all)
     moved(z_in.at[pl.ds(0, NZ - 1)], z_recv)
     running = jnp.zeros((PIECE, D), F32)
     for k in range(NZ):
@@ -301,7 +341,7 @@
         running = running + z_in[k].astype(F32)
 
     def c_start(k, held):
-        target = lax.rem(z + k, NZ)
+        target = other_plane(k, z)
 
         @pl.when(target > 0)
         def _():
@@ -312,7 +352,7 @@
 
         return held
 
-    lax.fori_loop(1, NZ, c_start, 0)
+    lax.fori_loop(0, NZ - 1, c_start, 0)
 
     @pl.when(z == 0)
     def _():
@@ -329,14 +369,14 @@
         done[step] = running.reshape(NS, PIECE, D).astype(BF16)
 
     def u_start(k, _):
-        x_to, s_to = lax.rem(x + k // NS, NX), lax.rem(s + lax.rem(k, NS), NS)
+        x_to, s_to = other(k, x, s)
         pltpu.make_async_remote_copy(
             src_ref=done.at[x_to, s_to], dst_ref=out.at[own], send_sem=u_send, recv_sem=u_recv,
             device_id=to(z * NX + x_to, s_to), device_id_type=MESH,
         ).start()
         return _
 
-    lax.fori_loop(1, NX * NS, u_start, 0)
+    lax.fori_loop(0, NX * NS - 1, u_start, 0)
     keep = pltpu.make_async_copy(done.at[x, s], out.at[own], own_sem)
     keep.start()
 
@@ -361,15 +401,16 @@
         part[step] = tile
 
     def p_start(k, _):
-        x_to, s_to = lax.rem(x + k // NS, NX), lax.rem(s + lax.rem(k, NS), NS)
+        x_to, s_to = other(k, x, s)
         pltpu.make_async_remote_copy(
             src_ref=part.at[x_to], dst_ref=parts.at[x * NS + s], send_sem=p_send, recv_sem=p_recv,
             device_id=to(z * NX + x_to, s_to), device_id_type=MESH,
         ).start()
         return _
 
-    lax.fori_loop(1, NX * NS, p_start, 0)
-    parts[x * NS + s] = part[x]
+    lax.fori_loop(0, NX * NS - 1, p_start, 0)
+    keep_part = pltpu.make_async_copy(part.at[x], parts.at[x * NS + s], own_part_sem)
+    keep_part.start()
 
     moved(temper.at[pl.ds(0, NX - 1)], temper_send)
     moved(mine.at[pl.ds(0, NX * NS - 1)], y_send)
@@ -393,11 +434,23 @@
         moved(carry.at[pl.ds(0, NZ - 2)], c_send)
 
     keep.wait()
+    keep_part.wait()
     moved(mine.at[pl.ds(0, NX * NS - 1)], u_send)
     moved(parts.at[pl.ds(0, NX * NS - 1)], p_send)
     moved(mine.at[pl.ds(0, NX * NS - 1)], u_recv)
     moved(parts.at[pl.ds(0, NX * NS - 1)], p_recv)
-    change_ref[0] = jnp.sum(jnp.sum(parts[...], axis=0)) * (1.0 / (NS * ROWS * D))
+
+
+def finish(rows_ref, parts_ref, out, change_ref, sem):
+    copies = [
+        pltpu.make_async_copy(rows_ref.at[pl.ds(i * 8, 8)], out.at[pl.ds(i * 8, 8)], sem.at[i])
+        for i in range(4)
+    ]
+    for copy in copies:
+        copy.start()
+    change_ref[0] = jnp.sum(jnp.sum(parts_ref[...], axis=0)) * (1.0 / (NS * ROWS * D))
+    for copy in copies:
+        copy.wait()
 
 
 def body(latents, timesteps, step_sizes, modulation, spatial_qkv, spatial_out, temporal_qkv, temporal_out):
@@ -410,11 +463,11 @@
         return pltpu.VMEM((count or (NX * NS,)) + (PIECE, D), BF16)
 
     table = modulation.shape[0]
-    updated, change = pl.pallas_call(
+    landed, parts = pl.pallas_call(
         kernel,
-        out_shape=(jax.ShapeDtypeStruct((NX * NS, PIECE, D), BF16), jax.ShapeDtypeStruct((1,), F32)),
+        out_shape=(jax.ShapeDtypeStruct((NX * NS, PIECE, D), BF16), jax.ShapeDtypeStruct((NX * NS, 8, 128), F32)),
         in_specs=[pl.BlockSpec(memory_space=pl.ANY)] * 8,
-        out_specs=(pl.BlockSpec(memory_space=pl.ANY), pl.BlockSpec(memory_space=pltpu.SMEM)),
+        out_specs=(pl.BlockSpec(memory_space=pl.ANY), pl.BlockSpec(memory_space=pl.ANY)),
         scratch_shapes=[
             pltpu.SMEM((1,), jnp.int32), pltpu.SMEM((1,), F32),
             pieces(), vmem(table, 6 * D),
@@ -424,12 +477,12 @@
             pieces(), pieces(), vmem(NX, 8, D, dtype=F32), pieces(NX + 1, NS),
             vmem(NX, STEP_ROWS, D, dtype=F32),
             pieces(NZ), pieces(NZ), pieces(NZ), pieces(NZ), pieces(NX, NS),
-            vmem(NX, 8, 128, dtype=F32), vmem(NX * NS, 8, 128, dtype=F32),
-            dma((8,)), dma, dma, dma, dma, dma, dma((3,)),
-            dma, dma, dma, dma, dma, dma, dma, dma, dma,
+            vmem(NX, 8, 128, dtype=F32),
+            dma((9,)), dma, dma, dma, dma, dma, dma((3,)),
+            dma, dma, dma, dma, dma, dma, dma, dma, dma, dma,
         ],
         compiler_params=pltpu.CompilerParams(
-            collective_id=0, has_side_effects=True, vmem_limit_bytes=56 * 1024 * 1024
+            collective_id=0, has_side_effects=True, vmem_limit_bytes=54000 * 1024
         ),
         cost_estimate=pl.CostEstimate(
             flops=2800000000, bytes_accessed=12000000, transcendentals=1000000
@@ -438,6 +491,13 @@
         latents.reshape(NX * NS, PIECE, D), timesteps, step_sizes, modulation,
         spatial_qkv.T, spatial_out, temporal_qkv.T, temporal_out,
     )
+    updated, change = pl.pallas_call(
+        finish,
+        out_shape=(jax.ShapeDtypeStruct(landed.shape, BF16), jax.ShapeDtypeStruct((1,), F32)),
+        in_specs=[pl.BlockSpec(memory_space=pl.ANY), pl.BlockSpec(memory_space=pltpu.VMEM)],
+        out_specs=(pl.BlockSpec(memory_space=pl.ANY), pl.BlockSpec(memory_space=pltpu.SMEM)),
+        scratch_shapes=[dma((4,))],
+    )(landed, parts)
     return updated.reshape(latents.shape), change
 
 

time: 59.3 us -> 79.4 us (1.34)
  the two profiles are of different devices: /device:TPU:33 before, /device:TPU:35 now
where the time goes in v5:
time: 79.4 us; the launch traced here: 79.2 us
  Pallas kernels  74.8 us (94%)
  local copies, waits for them, and re-layouts  2.48 us (3%)
  between operations  1.95 us (2%)
    pallas_call x1, Pallas kernels, body(): pl.pallas_call(kernel, out_shape=(jax.ShapeDtypeStruct((NX * NS, PIECE, D...  54.4 us
    pallas_call x1, Pallas kernels, body(): pl.pallas_call(finish, out_shape=(jax.ShapeDtypeStruct(landed.shape, BF16...  20.4 us
    unnamed x6, local copies, waits for them, and re-layouts  2.48 us

profile of v5, /device:TPU:35, one launch (start us, length us, event | category | flops | bytes accessed | tf_op | source)
XLA Modules:
  0.0 79.2 jit_solution(7297377713436114925)
XLA Ops:
  1.9 0.0 copy-start.1
  1.9 1.0 %copy-done.1 = bf16[32,6912]{1,0:T(8,128)(2,1)S(1)} copy-done((bf16[32,6912]{1,0:T(8,128)(2,1)S(1)}, bf16[32,6912]{1,0:T(8,128)(2,1)}, u32[]{:S(2)}) %copy-start.1) | copy-done | bytes 442392
  2.9 54.4 %shard_map.95 = (bf16[32,8,1152]{2,1,0:T(8,128)(2,1)S(1)}, f32[32,8,128]{2,1,0:T(8,128)S(1)}) custom-call(bf16[32,8,1152]{2,1,0:T(8,128)(2,1)} %bitcast.6, s32[1]{0:T(128)S(6)} %copy.10.time_hbm, f32[1]{0:T(128)S(6)} %copy.11.size_hbm, bf16[32,6912]{1,0:T(8,128)(2,1)S(1)} %copy-done.1, bf16[1728,1152]{1,0:T(8,128)(2,1)} %bitcast.4, ...), custom_call_target="tpu_custom_call" | custom-call | flops 2800000000 | bytes 12000000 | tf_op jit(solution)/shard_map/pallas_call | solution.py:466
  57.3 0.0 copy-start
  57.3 0.8 %copy-done = bf16[32,8,1152]{2,1,0:T(8,128)(2,1)} copy-done((bf16[32,8,1152]{2,1,0:T(8,128)(2,1)}, bf16[32,8,1152]{2,1,0:T(8,128)(2,1)S(1)}, u32[]{:S(2)}) %copy-start) | copy-done | bytes 589848
  58.1 0.0 copy-start.2
  58.1 0.7 copy-done.2
  58.8 20.4 %shard_map.96 = (bf16[32,8,1152]{2,1,0:T(8,128)(2,1)}, f32[1]{0:T(128)}) custom-call(bf16[32,8,1152]{2,1,0:T(8,128)(2,1)} %copy-done, f32[32,8,128]{2,1,0:T(8,128)} %copy-done.2), custom_call_target="tpu_custom_call" | custom-call | tf_op jit(solution)/shard_map/pallas_call | solution.py:494
Async XLA Ops:
  1.9 1.0 %copy-start.1 = (bf16[32,6912]{1,0:T(8,128)(2,1)S(1)}, bf16[32,6912]{1,0:T(8,128)(2,1)}, u32[]{:S(2)}) copy-start(bf16[32,6912]{1,0:T(8,128)(2,1)} %mod_hbm.1) | copy-start | bytes 1327108
  57.3 0.8 %copy-start = (bf16[32,8,1152]{2,1,0:T(8,128)(2,1)}, bf16[32,8,1152]{2,1,0:T(8,128)(2,1)S(1)}, u32[]{:S(2)}) copy-start(bf16[32,8,1152]{2,1,0:T(8,128)(2,1)S(1)} %get-tuple-element.6.rows_ref) | copy-start | bytes 1769476
  58.1 0.7 copy-start.2

commit v6 on v5

--- a/solution.py
+++ b/solution.py
@@ -96,8 +96,8 @@
     lat_hbm, time_hbm, size_hbm, mod_hbm, w1_hbm, o1_hbm, w2_hbm, o2_hbm,
     out, parts,
     time_ref, size_ref, lat, mod, w1, o1, w2, o2, cond, inputs, raw, scores, heads,
-    after, mine, temper, following, drift, total, z_in, carry, c_in, done, part,
-    local_sem, temper_send, temper_recv, y_send, y_recv, next_send, next_recv,
+    after, mine, temper, state, drift, total, z_in, carry, c_in, done, part,
+    local_sem, temper_send, temper_recv, y_send, y_recv, next_send, next_recv, forward_send, forward_recv,
     z_send, z_recv, c_send, c_recv, u_send, u_recv, p_send, p_recv, own_sem, own_part_sem,
 ):
     me = lax.axis_index("step")
@@ -137,14 +137,6 @@
 
     lax.fori_loop(1, NZ, greet_planes, 0)
 
-    @pl.when(z < NZ - 1)
-    def _():
-        def greet_next(k, held):
-            greet((z + 1) * NX, lax.rem(s + k, NS))
-            return held
-
-        lax.fori_loop(0, NS, greet_next, 0)
-
     loads[6].wait()
     loads[7].wait()
     loads[0].wait()
@@ -199,18 +191,35 @@
     attend(raw, heads, scores, (slice(0, ROWS),), None)
     loads[3].wait()
 
-    @pl.when(jnp.logical_and(x == 0, z > 0))
-    def _():
-        pl.semaphore_wait(barrier, 2 * NX * NS - 1 + NZ - 1)
-
-    @pl.when(jnp.logical_not(jnp.logical_and(x == 0, z > 0)))
-    def _():
-        pl.semaphore_wait(barrier, NX * NS - 1 + NZ - 1)
+    pl.semaphore_wait(barrier, NX * NS - 1 + NZ - 1)
 
     def place(x_at, s_at):
         return lax.rem(s_at, 2) * 16 + (s_at // 2) * 4 + x_at
 
     own = place(x, s)
+
+    def next_start(k, _):
+        x_to, s_to = other(k, x, s)
+        pltpu.make_async_remote_copy(
+            src_ref=lat.at[place(x_to, s_to)], dst_ref=state.at[x, s], send_sem=next_send, recv_sem=next_recv,
+            device_id=to(z * NX + x_to, s_to), device_id_type=MESH,
+        ).start()
+        return _
+
+    def next_all():
+        lax.fori_loop(0, NX * NS - 1, next_start, 0)
+        state[x, s] = lat[own]
+
+    def next_wait():
+        moved(mine.at[pl.ds(0, NX * NS - 1)], next_recv)
+
+    def forward():
+        @pl.when(z > 0)
+        def _():
+            pltpu.make_async_remote_copy(
+                src_ref=state.at[0], dst_ref=state.at[NX], send_sem=forward_send, recv_sem=forward_recv,
+                device_id=to(me - NX, s), device_id_type=MESH,
+            ).start()
 
     for k in range(1, NX):
         pltpu.make_async_remote_copy(
@@ -224,8 +233,8 @@
         shown = lax.dot_general(
             heads[:, rows].astype(BF16), o1[...], contract_first, preferred_element_type=F32
         )
-        state = lat[pieces].astype(F32).reshape(HALF, D)
-        after[pieces] = (state + vector(2) * shown).reshape(16, PIECE, D).astype(BF16)
+        latent = lat[pieces].astype(F32).reshape(HALF, D)
+        after[pieces] = (latent + vector(2) * shown).reshape(16, PIECE, D).astype(BF16)
 
         def y_start(k, _):
             x_to, y_to = chip(k, x, s // 2)
@@ -243,37 +252,7 @@
 
         lax.fori_loop(0, 16, y_start, 0)
     mine[x * NS + s] = after[own]
-
-    first = me == 0
-    plane = jnp.where(jnp.logical_and(x == 0, z > 0), z - 1, z)
-    slot = jnp.where(first, NX, lax.rem(x + NX - 1, NX))
-    kind = jnp.where(first, 2, jnp.where(x == 0, 1, 0))
-
-    def next_start(k, _):
-        x_to, s_to = other(k, x, s)
-        pltpu.make_async_remote_copy(
-            src_ref=lat.at[place(x_to, s_to)], dst_ref=following.at[slot, s],
-            send_sem=next_send, recv_sem=next_recv.at[kind],
-            device_id=to(plane * NX + x_to, s_to), device_id_type=MESH,
-        ).start()
-        return _
-
-    def next_all():
-        lax.fori_loop(0, NX * NS - 1, next_start, 0)
-
-        @pl.when(plane != z)
-        def _():
-            next_start(NX * NS - 1, 0)
-
-        @pl.when(plane == z)
-        def _():
-            following[slot, s] = lat[own]
-
-    pl.when(first)(next_all)
-
-    @pl.when(z == NZ - 1)
-    def _():
-        following[NX - 1] = jnp.zeros(following.shape[1:], BF16)
+    next_all()
 
     loads[4].wait()
     loads[5].wait()
@@ -302,23 +281,16 @@
         )
         for i in range(2):
             step = half * 2 + i
-            state = mine[step * NS : (step + 1) * NS].astype(F32).reshape(STEP_ROWS, D)
+            rows_in = mine[step * NS : (step + 1) * NS].astype(F32).reshape(STEP_ROWS, D)
             drift[step] = (
-                state * temper[step, 3:4, :]
+                rows_in * temper[step, 3:4, :]
                 + temper[step, 2:3, :] * shown[i * STEP_ROWS : (i + 1) * STEP_ROWS]
             )
 
     @pl.when(z == 0)
     def _():
-        @pl.when(first)
-        def _():
-            moved(following.at[NX, pl.ds(0, NS - 1)], next_recv.at[2])
-
-        @pl.when(jnp.logical_not(first))
-        def _():
-            moved(following.at[NX], next_recv.at[2])
-
-        drift[0] = drift[0] + following[NX].astype(F32).reshape(STEP_ROWS, D)
+        next_wait()
+        drift[0] = drift[0] + state[0].astype(F32).reshape(STEP_ROWS, D)
 
     everything = drift[0] + drift[1] + drift[2] + drift[3]
     total[...] = everything.reshape(NS, PIECE, D).astype(BF16)
@@ -333,7 +305,6 @@
 
     lax.fori_loop(0, NZ - 1, z_start, 0)
     z_in[z] = total[z]
-    pl.when(jnp.logical_not(first))(next_all)
     moved(z_in.at[pl.ds(0, NZ - 1)], z_recv)
     running = jnp.zeros((PIECE, D), F32)
     for k in range(NZ):
@@ -353,6 +324,8 @@
         return held
 
     lax.fori_loop(0, NZ - 1, c_start, 0)
+    pl.when(z > 0)(next_wait)
+    forward()
 
     @pl.when(z == 0)
     def _():
@@ -380,20 +353,16 @@
     keep = pltpu.make_async_copy(done.at[x, s], out.at[own], own_sem)
     keep.start()
 
-    @pl.when(x == 0)
-    def _():
-        moved(following.at[pl.ds(0, NX - 1)], next_recv.at[0])
-
-    @pl.when(x > 0)
-    def _():
-        moved(mine.at[pl.ds(0, (NX - 1) * NS - 1)], next_recv.at[0])
-
     @pl.when(z < NZ - 1)
     def _():
-        moved(following.at[0], next_recv.at[1])
+        moved(state.at[NX], forward_recv)
+
+    @pl.when(z == NZ - 1)
+    def _():
+        state[NX] = jnp.zeros(state.shape[1:], BF16)
 
     for step in range(NX):
-        difference = done[step].astype(F32) - following[step].astype(F32)
+        difference = done[step].astype(F32) - state[step + 1].astype(F32)
         squares = jnp.sum(difference * difference, axis=0)
         tile = squares[:, :128]
         for t in range(1, D // 128):
@@ -415,13 +384,11 @@
     moved(temper.at[pl.ds(0, NX - 1)], temper_send)
     moved(mine.at[pl.ds(0, NX * NS - 1)], y_send)
 
-    @pl.when(plane != z)
-    def _():
-        moved(mine, next_send)
-
-    @pl.when(plane == z)
-    def _():
-        moved(mine.at[pl.ds(0, NX * NS - 1)], next_send)
+    moved(mine.at[pl.ds(0, NX * NS - 1)], next_send)
+
+    @pl.when(z > 0)
+    def _():
+        moved(state.at[0], forward_send)
 
     moved(z_in.at[pl.ds(0, NZ - 1)], z_send)
 
@@ -478,7 +445,7 @@
             vmem(NX, STEP_ROWS, D, dtype=F32),
             pieces(NZ), pieces(NZ), pieces(NZ), pieces(NZ), pieces(NX, NS),
             vmem(NX, 8, 128, dtype=F32),
-            dma((9,)), dma, dma, dma, dma, dma, dma((3,)),
+            dma((9,)), dma, dma, dma, dma, dma, dma, dma, dma,
             dma, dma, dma, dma, dma, dma, dma, dma, dma, dma,
         ],
         compiler_params=pltpu.CompilerParams(
@@ -497,6 +464,7 @@
         in_specs=[pl.BlockSpec(memory_space=pl.ANY), pl.BlockSpec(memory_space=pltpu.VMEM)],
         out_specs=(pl.BlockSpec(memory_space=pl.ANY), pl.BlockSpec(memory_space=pltpu.SMEM)),
         scratch_shapes=[dma((4,))],
+        compiler_params=pltpu.CompilerParams(vmem_limit_bytes=4 * 1024 * 1024),
     )(landed, parts)
     return updated.reshape(latents.shape), change
 

time: 79.4 us -> 51.3 us (0.65)
  the two profiles are of different devices: /device:TPU:35 before, /device:TPU:33 now
where the time goes in v6:
time: 51.3 us; the launch traced here: 50.5 us
  Pallas kernels  47.5 us (93%)
  between operations  1.94 us (4%)
  local copies, waits for them, and re-layouts  1.01 us (2%)
    pallas_call x1, Pallas kernels, body(): pl.pallas_call(kernel, out_shape=(jax.ShapeDtypeStruct((NX * NS, PIECE, D...  46.2 us
    pallas_call x1, Pallas kernels, body(): pl.pallas_call(finish, out_shape=(jax.ShapeDtypeStruct(landed.shape, BF16...  1.36 us

profile of v6, /device:TPU:33, one launch (start us, length us, event | category | flops | bytes accessed | tf_op | source)
XLA Modules:
  0.0 50.5 jit_solution(8046517600786345461)
XLA Ops:
  1.9 0.0 copy-start
  1.9 1.0 %copy-done = bf16[32,6912]{1,0:T(8,128)(2,1)S(1)} copy-done((bf16[32,6912]{1,0:T(8,128)(2,1)S(1)}, bf16[32,6912]{1,0:T(8,128)(2,1)}, u32[]{:S(2)}) %copy-start) | copy-done | bytes 442392
  2.9 46.2 %shard_map.95 = (bf16[32,8,1152]{2,1,0:T(8,128)(2,1)S(1)}, f32[32,8,128]{2,1,0:T(8,128)S(1)}) custom-call(bf16[32,8,1152]{2,1,0:T(8,128)(2,1)} %bitcast.6, s32[1]{0:T(128)S(6)} %copy.10.time_hbm, f32[1]{0:T(128)S(6)} %copy.11.size_hbm, bf16[32,6912]{1,0:T(8,128)(2,1)S(1)} %copy-done, bf16[1728,1152]{1,0:T(8,128)(2,1)} %bitcast.4, bf16[576,1152]{1,0:T(8,128)(2,1)} %o1_hbm.1, ...), custom_call_target="tpu_custom_call" | custom-call | flops 2800000000 | bytes 12000000 | tf_op jit(solution)/shard_map/pallas_call | solution.py:433
  49.1 1.4 %shard_map.96 = (bf16[32,8,1152]{2,1,0:T(8,128)(2,1)}, f32[1]{0:T(128)}) custom-call(bf16[32,8,1152]{2,1,0:T(8,128)(2,1)S(1)} %get-tuple-element.6.rows_ref, f32[32,8,128]{2,1,0:T(8,128)S(1)} %get-tuple-element.7.parts_ref), custom_call_target="tpu_custom_call" | custom-call | tf_op jit(solution)/shard_map/pallas_call | solution.py:461
Async XLA Ops:
  1.9 1.0 %copy-start = (bf16[32,6912]{1,0:T(8,128)(2,1)S(1)}, bf16[32,6912]{1,0:T(8,128)(2,1)}, u32[]{:S(2)}) copy-start(bf16[32,6912]{1,0:T(8,128)(2,1)} %mod_hbm.1) | copy-start | bytes 1327108

commit v7 on v6

--- a/solution.py
+++ b/solution.py
@@ -94,7 +94,7 @@
 
 def kernel(
     lat_hbm, time_hbm, size_hbm, mod_hbm, w1_hbm, o1_hbm, w2_hbm, o2_hbm,
-    out, parts,
+    out_a, out_b, parts,
     time_ref, size_ref, lat, mod, w1, o1, w2, o2, cond, inputs, raw, scores, heads,
     after, mine, temper, state, drift, total, z_in, carry, c_in, done, part,
     local_sem, temper_send, temper_recv, y_send, y_recv, next_send, next_recv, forward_send, forward_recv,
@@ -298,32 +298,33 @@
     def z_start(k, _):
         target = other_plane(k, z)
         pltpu.make_async_remote_copy(
-            src_ref=total.at[target], dst_ref=z_in.at[z], send_sem=z_send, recv_sem=z_recv,
+            src_ref=total.at[target], dst_ref=z_in.at[z], send_sem=z_send, recv_sem=z_recv.at[z],
             device_id=to(target * NX + x, s), device_id_type=MESH,
         ).start()
         return _
 
-    lax.fori_loop(0, NZ - 1, z_start, 0)
-    z_in[z] = total[z]
-    moved(z_in.at[pl.ds(0, NZ - 1)], z_recv)
+    @pl.when(z < NZ - 1)
+    def _():
+        lax.fori_loop(0, NZ - 1, z_start, 0)
+        z_in[z] = total[z]
+
     running = jnp.zeros((PIECE, D), F32)
-    for k in range(NZ):
-        carry[k] = running.astype(BF16)
+    for k in range(NZ - 1):
+
+        @pl.when(z != k)
+        def _():
+            moved(z_in.at[k], z_recv.at[k])
+
         running = running + z_in[k].astype(F32)
-
-    def c_start(k, held):
-        target = other_plane(k, z)
-
-        @pl.when(target > 0)
+        carry[k + 1] = running.astype(BF16)
+
+        @pl.when(z != k + 1)
         def _():
             pltpu.make_async_remote_copy(
-                src_ref=carry.at[target], dst_ref=c_in.at[z], send_sem=c_send, recv_sem=c_recv,
-                device_id=to(target * NX + x, s), device_id_type=MESH,
+                src_ref=carry.at[k + 1], dst_ref=c_in.at[z], send_sem=c_send, recv_sem=c_recv,
+                device_id=to((k + 1) * NX + x, s), device_id_type=MESH,
             ).start()
 
-        return held
-
-    lax.fori_loop(0, NZ - 1, c_start, 0)
     pl.when(z > 0)(next_wait)
     forward()
 
@@ -341,17 +342,27 @@
         running = running + drift[step]
         done[step] = running.reshape(NS, PIECE, D).astype(BF16)
 
-    def u_start(k, _):
-        x_to, s_to = other(k, x, s)
-        pltpu.make_async_remote_copy(
-            src_ref=done.at[x_to, s_to], dst_ref=out.at[own], send_sem=u_send, recv_sem=u_recv,
-            device_id=to(z * NX + x_to, s_to), device_id_type=MESH,
-        ).start()
-        return _
-
-    lax.fori_loop(0, NX * NS - 1, u_start, 0)
-    keep = pltpu.make_async_copy(done.at[x, s], out.at[own], own_sem)
-    keep.start()
+    def rows_out(out, at):
+        def u_start(k, _):
+            x_to, s_to = other(k, x, s)
+            pltpu.make_async_remote_copy(
+                src_ref=done.at[x_to, s_to], dst_ref=out.at[at], send_sem=u_send, recv_sem=u_recv,
+                device_id=to(z * NX + x_to, s_to), device_id_type=MESH,
+            ).start()
+            return _
+
+        lax.fori_loop(0, NX * NS - 1, u_start, 0)
+        pltpu.make_async_copy(done.at[x, s], out.at[at], own_sem).start()
+
+    at = lax.rem(own, 16)
+
+    @pl.when(lax.rem(s, 2) == 0)
+    def _():
+        rows_out(out_a, at)
+
+    @pl.when(lax.rem(s, 2) == 1)
+    def _():
+        rows_out(out_b, at)
 
     @pl.when(z < NZ - 1)
     def _():
@@ -390,7 +401,10 @@
     def _():
         moved(state.at[0], forward_send)
 
-    moved(z_in.at[pl.ds(0, NZ - 1)], z_send)
+
+    @pl.when(z < NZ - 1)
+    def _():
+        moved(z_in.at[pl.ds(0, NZ - 1)], z_send)
 
     @pl.when(z == 0)
     def _():
@@ -400,7 +414,7 @@
     def _():
         moved(carry.at[pl.ds(0, NZ - 2)], c_send)
 
-    keep.wait()
+    moved(mine.at[0], own_sem)
     keep_part.wait()
     moved(mine.at[pl.ds(0, NX * NS - 1)], u_send)
     moved(parts.at[pl.ds(0, NX * NS - 1)], p_send)
@@ -408,10 +422,10 @@
     moved(parts.at[pl.ds(0, NX * NS - 1)], p_recv)
 
 
-def finish(rows_ref, parts_ref, out, change_ref, sem):
+def finish(first_ref, second_ref, parts_ref, out, change_ref, sem):
     copies = [
-        pltpu.make_async_copy(rows_ref.at[pl.ds(i * 8, 8)], out.at[pl.ds(i * 8, 8)], sem.at[i])
-        for i in range(4)
+        pltpu.make_async_copy(ref, out.at[pl.ds(i * 16, 16)], sem.at[i])
+        for i, ref in enumerate((first_ref, second_ref))
     ]
     for copy in copies:
         copy.start()
@@ -429,12 +443,13 @@
     def pieces(*count):
         return pltpu.VMEM((count or (NX * NS,)) + (PIECE, D), BF16)
 
+    half_rows = jax.ShapeDtypeStruct((NX * NS // 2, PIECE, D), BF16)
     table = modulation.shape[0]
-    landed, parts = pl.pallas_call(
+    first, second, parts = pl.pallas_call(
         kernel,
-        out_shape=(jax.ShapeDtypeStruct((NX * NS, PIECE, D), BF16), jax.ShapeDtypeStruct((NX * NS, 8, 128), F32)),
+        out_shape=(half_rows, half_rows, jax.ShapeDtypeStruct((NX * NS, 8, 128), F32)),
         in_specs=[pl.BlockSpec(memory_space=pl.ANY)] * 8,
-        out_specs=(pl.BlockSpec(memory_space=pl.ANY), pl.BlockSpec(memory_space=pl.ANY)),
+        out_specs=(pl.BlockSpec(memory_space=pl.ANY),) * 3,
         scratch_shapes=[
             pltpu.SMEM((1,), jnp.int32), pltpu.SMEM((1,), F32),
             pieces(), vmem(table, 6 * D),
@@ -446,10 +461,10 @@
             pieces(NZ), pieces(NZ), pieces(NZ), pieces(NZ), pieces(NX, NS),
             vmem(NX, 8, 128, dtype=F32),
             dma((9,)), dma, dma, dma, dma, dma, dma, dma, dma,
-            dma, dma, dma, dma, dma, dma, dma, dma, dma, dma,
+            dma, dma((NZ,)), dma, dma, dma, dma, dma, dma, dma, dma,
         ],
         compiler_params=pltpu.CompilerParams(
-            collective_id=0, has_side_effects=True, vmem_limit_bytes=54000 * 1024
+            collective_id=0, has_side_effects=True, vmem_limit_bytes=54374 * 1024
         ),
         cost_estimate=pl.CostEstimate(
             flops=2800000000, bytes_accessed=12000000, transcendentals=1000000
@@ -460,12 +475,12 @@
     )
     updated, change = pl.pallas_call(
         finish,
-        out_shape=(jax.ShapeDtypeStruct(landed.shape, BF16), jax.ShapeDtypeStruct((1,), F32)),
-        in_specs=[pl.BlockSpec(memory_space=pl.ANY), pl.BlockSpec(memory_space=pltpu.VMEM)],
+        out_shape=(jax.ShapeDtypeStruct((NX * NS, PIECE, D), BF16), jax.ShapeDtypeStruct((1,), F32)),
+        in_specs=[pl.BlockSpec(memory_space=pl.ANY)] * 2 + [pl.BlockSpec(memory_space=pltpu.VMEM)],
         out_specs=(pl.BlockSpec(memory_space=pl.ANY), pl.BlockSpec(memory_space=pltpu.SMEM)),
-        scratch_shapes=[dma((4,))],
+        scratch_shapes=[dma((2,))],
         compiler_params=pltpu.CompilerParams(vmem_limit_bytes=4 * 1024 * 1024),
-    )(landed, parts)
+    )(first, second, parts)
     return updated.reshape(latents.shape), change
 
 

time: 51.3 us -> 48.8 us (0.951); the launches traced: 50.5 us -> 48.7 us
  local copies, waits for them, and re-layouts: 1.01 us -> 0 us
  Pallas kernels: 47.5 us -> 46.7 us
    unnamed x2 -> x0, local copies, waits for them, and re-layouts: 1.01 us -> none
    pallas_call x2, Pallas kernels: 47.5 us -> 46.7 us  [the longest x1 45.4 us: body(): pl.pallas_call(kernel, out_shape=(half_rows, half_rows, jax.ShapeDtypeStr...]
where the time goes in v7:
time: 48.8 us; the launch traced here: 48.7 us
  Pallas kernels  46.7 us (96%)
  between operations  1.93 us (4%)
    pallas_call x1, Pallas kernels, body(): pl.pallas_call(kernel, out_shape=(half_rows, half_rows, jax.ShapeDtypeStr...  45.4 us
    pallas_call x1, Pallas kernels, body(): pl.pallas_call(finish, out_shape=(jax.ShapeDtypeStruct((NX * NS, PIECE, D...  1.35 us

profile of v7, /device:TPU:33, one launch (start us, length us, event | category | flops | bytes accessed | tf_op | source)
XLA Modules:
  0.0 48.7 jit_solution(15808339020367696260)
XLA Ops:
  1.9 45.4 %shard_map.95 = (bf16[16,8,1152]{2,1,0:T(8,128)(2,1)S(1)}, bf16[16,8,1152]{2,1,0:T(8,128)(2,1)S(1)}, f32[32,8,128]{2,1,0:T(8,128)S(1)}) custom-call(bf16[32,8,1152]{2,1,0:T(8,128)(2,1)} %bitcast.6, s32[1]{0:T(128)S(6)} %copy.10.time_hbm, f32[1]{0:T(128)S(6)} %copy.11.size_hbm, bf16[32,6912]{1,0:T(8,128)(2,1)} %mod_hbm.1, bf16[1728,1152]{1,0:T(8,128)(2,1)} %bitcast.4, ...), custom_call_target="tpu_custom_call" | custom-call | flops 2800000000 | bytes 12000000 | tf_op jit(solution)/shard_map/pallas_call | solution.py:448
  47.3 1.4 %shard_map.96 = (bf16[32,8,1152]{2,1,0:T(8,128)(2,1)}, f32[1]{0:T(128)}) custom-call(bf16[16,8,1152]{2,1,0:T(8,128)(2,1)S(1)} %get-tuple-element.7.first_ref, bf16[16,8,1152]{2,1,0:T(8,128)(2,1)S(1)} %get-tuple-element.8.second_ref, f32[32,8,128]{2,1,0:T(8,128)S(1)} %get-tuple-element.9.parts_ref), custom_call_target="tpu_custom_call" | custom-call | tf_op jit(solution)/shard_map/pallas_call | solution.py:476

commit v8 on v7

--- a/solution.py
+++ b/solution.py
@@ -23,6 +23,7 @@
 NX = 4
 NZ = 8
 NS = 8
+GROUP = 4
 STEP_ROWS = NS * PIECE
 EPS = 1e-6
 LOG2E = 1.4426950408889634
@@ -46,10 +47,6 @@
 def other(j, x, s):
     x_to, y_to = chip(j // 2, x, s // 2)
     return x_to, y_to * 2 + lax.rem(s + 1 + lax.rem(j, 2), 2)
-
-
-def other_plane(j, z):
-    return lax.rem(z + NZ // 2 + (1 - 2 * lax.rem(j, 2)) * ((j + 1) // 2), NZ)
 
 
 def layer_norm(values):
@@ -98,7 +95,7 @@
     time_ref, size_ref, lat, mod, w1, o1, w2, o2, cond, inputs, raw, scores, heads,
     after, mine, temper, state, drift, total, z_in, carry, c_in, done, part,
     local_sem, temper_send, temper_recv, y_send, y_recv, next_send, next_recv, forward_send, forward_recv,
-    z_send, z_recv, c_send, c_recv, u_send, u_recv, p_send, p_recv, own_sem, own_part_sem,
+    z_send, z_recv, c_send, c_recv, u_sent, u_recv, p_send, p_recv, own_sem, own_part_sem,
 ):
     me = lax.axis_index("step")
     s = lax.axis_index("seq")
@@ -295,35 +292,61 @@
     everything = drift[0] + drift[1] + drift[2] + drift[3]
     total[...] = everything.reshape(NS, PIECE, D).astype(BF16)
 
-    def z_start(k, _):
-        target = other_plane(k, z)
+    def pair(holder):
+        return lax.rem(holder + x + s // 2, GROUP)
+
+    def z_send_to(target):
         pltpu.make_async_remote_copy(
-            src_ref=total.at[target], dst_ref=z_in.at[z], send_sem=z_send, recv_sem=z_recv.at[z],
+            src_ref=total.at[pl.ds(2 * pair(target % GROUP), 2)], dst_ref=z_in.at[z],
+            send_sem=z_send, recv_sem=z_recv.at[z],
             device_id=to(target * NX + x, s), device_id_type=MESH,
         ).start()
-        return _
-
-    @pl.when(z < NZ - 1)
-    def _():
-        lax.fori_loop(0, NZ - 1, z_start, 0)
-        z_in[z] = total[z]
-
-    running = jnp.zeros((PIECE, D), F32)
-    for k in range(NZ - 1):
-
+
+    for target in (4, 7, 5, 6, 0, 1, 2, 3):
+        needed = z < NZ - 1 if target >= GROUP else z < GROUP - 1
+
+        @pl.when(jnp.logical_and(needed, z != target))
+        def _():
+            z_send_to(target)
+
+    member = lax.rem(z, GROUP)
+    z_in[z] = total[pl.ds(2 * pair(member), 2)]
+
+    def z_wait(k):
         @pl.when(z != k)
         def _():
             moved(z_in.at[k], z_recv.at[k])
 
-        running = running + z_in[k].astype(F32)
-        carry[k + 1] = running.astype(BF16)
-
-        @pl.when(z != k + 1)
+    def c_send_to(target):
+        @pl.when(z != target)
         def _():
             pltpu.make_async_remote_copy(
-                src_ref=carry.at[k + 1], dst_ref=c_in.at[z], send_sem=c_send, recv_sem=c_recv,
-                device_id=to((k + 1) * NX + x, s), device_id_type=MESH,
+                src_ref=carry.at[target], dst_ref=c_in.at[pl.ds(2 * pair(member), 2)], send_sem=c_send, recv_sem=c_recv.at[member],
+                device_id=to(target * NX + x, s), device_id_type=MESH,
             ).start()
+
+        @pl.when(z == target)
+        def _():
+            c_in[pl.ds(2 * pair(member), 2)] = carry[target]
+
+    @pl.when(z < GROUP)
+    def _():
+        running = jnp.zeros((2, PIECE, D), F32)
+        for k in range(GROUP - 1):
+            z_wait(k)
+            running = running + z_in[k].astype(F32)
+            carry[k + 1] = running.astype(BF16)
+            c_send_to(k + 1)
+
+    @pl.when(z >= GROUP)
+    def _():
+        running = jnp.zeros((2, PIECE, D), F32)
+        for k in range(NZ - 1):
+            z_wait(k)
+            running = running + z_in[k].astype(F32)
+            if k + 1 >= GROUP:
+                carry[k + 1] = running.astype(BF16)
+                c_send_to(k + 1)
 
     pl.when(z > 0)(next_wait)
     forward()
@@ -332,37 +355,50 @@
     def _():
         c_in[...] = jnp.zeros(c_in.shape, BF16)
 
-    @pl.when(z > 0)
-    def _():
-        c_in[z] = carry[z]
-        moved(c_in.at[pl.ds(0, NZ - 1)], c_recv)
-
-    running = c_in[...].astype(F32).reshape(STEP_ROWS, D)
-    for step in range(NX):
-        running = running + drift[step]
-        done[step] = running.reshape(NS, PIECE, D).astype(BF16)
-
-    def rows_out(out, at):
-        def u_start(k, _):
-            x_to, s_to = other(k, x, s)
-            pltpu.make_async_remote_copy(
-                src_ref=done.at[x_to, s_to], dst_ref=out.at[at], send_sem=u_send, recv_sem=u_recv,
-                device_id=to(z * NX + x_to, s_to), device_id_type=MESH,
-            ).start()
-            return _
-
-        lax.fori_loop(0, NX * NS - 1, u_start, 0)
-        pltpu.make_async_copy(done.at[x, s], out.at[at], own_sem).start()
-
-    at = lax.rem(own, 16)
-
-    @pl.when(lax.rem(s, 2) == 0)
-    def _():
-        rows_out(out_a, at)
-
-    @pl.when(lax.rem(s, 2) == 1)
-    def _():
-        rows_out(out_b, at)
+    own_slot = lax.rem(own, 16)
+
+    def u_send(x_to, frame):
+        for core, out in enumerate((out_a, out_b)):
+
+            @pl.when(lax.rem(s, 2) == core)
+            def _():
+                pltpu.make_async_remote_copy(
+                    src_ref=done.at[x_to, frame], dst_ref=out.at[own_slot], send_sem=u_sent, recv_sem=u_recv,
+                    device_id=to(z * NX + x_to, frame), device_id_type=MESH,
+                ).start()
+
+    def u_frames(j, kept):
+        holder = lax.rem(member + j, GROUP)
+        frames = pl.ds(2 * pair(holder), 2)
+
+        @pl.when(jnp.logical_and(z > 0, j > 0))
+        def _():
+            moved(c_in.at[frames], c_recv.at[holder])
+
+        carried = c_in[frames].astype(F32).reshape(2 * PIECE, D)
+        for step in range(NX):
+            rows = pl.ds(pl.multiple_of(pair(holder) * 2 * PIECE, 2 * PIECE), 2 * PIECE)
+            carried = carried + drift[step, rows, :]
+            done[step, frames] = carried.reshape(2, PIECE, D).astype(BF16)
+
+        def u_start(k, held):
+            x_to, frame = lax.rem(x + 2 + k // 2, NX), 2 * pair(holder) + lax.rem(s + 1 + k, 2)
+
+            @pl.when(jnp.logical_or(x_to != x, frame != s))
+            def _():
+                u_send(x_to, frame)
+
+            return held
+
+        lax.fori_loop(0, 2 * NX, u_start, 0)
+        return kept
+
+    lax.fori_loop(0, GROUP, u_frames, 0)
+    for core, out in enumerate((out_a, out_b)):
+
+        @pl.when(lax.rem(s, 2) == core)
+        def _():
+            pltpu.make_async_copy(done.at[x, s], out.at[own_slot], own_sem).start()
 
     @pl.when(z < NZ - 1)
     def _():
@@ -378,7 +414,7 @@
         tile = squares[:, :128]
         for t in range(1, D // 128):
             tile = tile + squares[:, t * 128 : (t + 1) * 128]
-        part[step] = tile
+        part[step] = jnp.sum(tile, axis=0, keepdims=True)
 
     def p_start(k, _):
         x_to, s_to = other(k, x, s)
@@ -402,21 +438,31 @@
         moved(state.at[0], forward_send)
 
 
-    @pl.when(z < NZ - 1)
-    def _():
-        moved(z_in.at[pl.ds(0, NZ - 1)], z_send)
-
-    @pl.when(z == 0)
-    def _():
-        moved(carry.at[pl.ds(0, NZ - 1)], c_send)
-
-    @pl.when(z > 0)
-    def _():
-        moved(carry.at[pl.ds(0, NZ - 2)], c_send)
+    @pl.when(z < GROUP - 1)
+    def _():
+        moved(z_in.at[pl.ds(0, 7)], z_send)
+
+    @pl.when(z == GROUP - 1)
+    def _():
+        moved(z_in.at[pl.ds(0, 4)], z_send)
+
+    @pl.when(jnp.logical_and(z >= GROUP, z < NZ - 1))
+    def _():
+        moved(z_in.at[pl.ds(0, 3)], z_send)
+
+    few = jnp.logical_and(z > 0, z < GROUP)
+
+    @pl.when(few)
+    def _():
+        moved(carry.at[pl.ds(0, 2)], c_send)
+
+    @pl.when(jnp.logical_not(few))
+    def _():
+        moved(carry.at[pl.ds(0, 3)], c_send)
 
     moved(mine.at[0], own_sem)
     keep_part.wait()
-    moved(mine.at[pl.ds(0, NX * NS - 1)], u_send)
+    moved(mine.at[pl.ds(0, NX * NS - 1)], u_sent)
     moved(parts.at[pl.ds(0, NX * NS - 1)], p_send)
     moved(mine.at[pl.ds(0, NX * NS - 1)], u_recv)
     moved(parts.at[pl.ds(0, NX * NS - 1)], p_recv)
@@ -447,7 +493,7 @@
     table = modulation.shape[0]
     first, second, parts = pl.pallas_call(
         kernel,
-        out_shape=(half_rows, half_rows, jax.ShapeDtypeStruct((NX * NS, 8, 128), F32)),
+        out_shape=(half_rows, half_rows, jax.ShapeDtypeStruct((NX * NS, 1, 128), F32)),
         in_specs=[pl.BlockSpec(memory_space=pl.ANY)] * 8,
         out_specs=(pl.BlockSpec(memory_space=pl.ANY),) * 3,
         scratch_shapes=[
@@ -458,10 +504,10 @@
             vmem(3 * E, ROWS, dtype=F32), vmem(2, ROWS, ROWS, dtype=F32), vmem(E, ROWS, dtype=F32),
             pieces(), pieces(), vmem(NX, 8, D, dtype=F32), pieces(NX + 1, NS),
             vmem(NX, STEP_ROWS, D, dtype=F32),
-            pieces(NZ), pieces(NZ), pieces(NZ), pieces(NZ), pieces(NX, NS),
-            vmem(NX, 8, 128, dtype=F32),
+            pieces(NZ), pieces(NZ, 2), pieces(NZ, 2), pieces(NZ), pieces(NX, NS),
+            vmem(NX, 1, 128, dtype=F32),
             dma((9,)), dma, dma, dma, dma, dma, dma, dma, dma,
-            dma, dma((NZ,)), dma, dma, dma, dma, dma, dma, dma, dma,
+            dma, dma((NZ,)), dma, dma((GROUP,)), dma, dma, dma, dma, dma, dma,
         ],
         compiler_params=pltpu.CompilerParams(
             collective_id=0, has_side_effects=True, vmem_limit_bytes=54374 * 1024

time: 48.8 us -> 45.4 us (0.930)
  Pallas kernels: 46.7 us -> 43.3 us
    pallas_call x1, Pallas kernels: 45.4 us -> 42 us  [body(): pl.pallas_call(kernel, out_shape=(half_rows, half_rows, jax.ShapeDtypeStr...]
where the time goes in v8:
time: 45.4 us; the launch traced here: 45.3 us
  Pallas kernels  43.3 us (95%)
  between operations  1.93 us (4%)
    pallas_call x1, Pallas kernels, body(): pl.pallas_call(kernel, out_shape=(half_rows, half_rows, jax.ShapeDtypeStr...  42 us
    pallas_call x1, Pallas kernels, body(): pl.pallas_call(finish, out_shape=(jax.ShapeDtypeStruct((NX * NS, PIECE, D...  1.35 us

profile of v8, /device:TPU:33, one launch (start us, length us, event | category | flops | bytes accessed | tf_op | source)
XLA Modules:
  0.0 45.3 jit_solution(8683423552552434651)
XLA Ops:
  1.9 42.0 %shard_map.95 = (bf16[16,8,1152]{2,1,0:T(8,128)(2,1)S(1)}, bf16[16,8,1152]{2,1,0:T(8,128)(2,1)S(1)}, f32[32,1,128]{2,1,0:T(1,128)S(1)}) custom-call(bf16[32,8,1152]{2,1,0:T(8,128)(2,1)} %bitcast.6, s32[1]{0:T(128)S(6)} %copy.10.time_hbm, f32[1]{0:T(128)S(6)} %copy.11.size_hbm, bf16[32,6912]{1,0:T(8,128)(2,1)} %mod_hbm.1, bf16[1728,1152]{1,0:T(8,128)(2,1)} %bitcast.4, ...), custom_call_target="tpu_custom_call" | custom-call | flops 2800000000 | bytes 12000000 | tf_op jit(solution)/shard_map/pallas_call | solution.py:494
  43.9 1.4 %shard_map.96 = (bf16[32,8,1152]{2,1,0:T(8,128)(2,1)}, f32[1]{0:T(128)}) custom-call(bf16[16,8,1152]{2,1,0:T(8,128)(2,1)S(1)} %get-tuple-element.7.first_ref, bf16[16,8,1152]{2,1,0:T(8,128)(2,1)S(1)} %get-tuple-element.8.second_ref, f32[32,1,128]{2,1,0:T(1,128)S(1)} %get-tuple-element.9.parts_ref), custom_call_target="tpu_custom_call" | custom-call | tf_op jit(solution)/shard_map/pallas_call | solution.py:522

commit v9 on v8

--- a/solution.py
+++ b/solution.py
@@ -249,12 +249,13 @@
 
         lax.fori_loop(0, 16, y_start, 0)
     mine[x * NS + s] = after[own]
-    next_all()
+    pl.when(z < GROUP)(next_all)
 
     loads[4].wait()
     loads[5].wait()
     moved(temper.at[pl.ds(0, NX - 1)], temper_recv)
     moved(mine.at[pl.ds(0, NX * NS - 1)], y_recv)
+    pl.when(z >= GROUP)(next_all)
 
     def temporal_in(i, _):
         normal_in(mine, i, temper[i, 0:1, :], temper[i, 1:2, :], NS)
@@ -302,7 +303,7 @@
             device_id=to(target * NX + x, s), device_id_type=MESH,
         ).start()
 
-    for target in (4, 7, 5, 6, 0, 1, 2, 3):
+    for target in (0, 3, 1, 2, 4, 7, 5, 6):
         needed = z < NZ - 1 if target >= GROUP else z < GROUP - 1
 
         @pl.when(jnp.logical_and(needed, z != target))

time: 45.4 us -> 45.5 us (level); the launches traced: 45.3 us -> 44.7 us
  Pallas kernels: 43.3 us -> 42.8 us
    pallas_call x1, Pallas kernels: 42 us -> 41.4 us  [body(): pl.pallas_call(kernel, out_shape=(half_rows, half_rows, jax.ShapeDtypeStr...]
where the time goes in v9:
time: 45.5 us; the launch traced here: 44.7 us
  Pallas kernels  42.8 us (94%)
  between operations  1.93 us (4%)
    pallas_call x1, Pallas kernels, body(): pl.pallas_call(kernel, out_shape=(half_rows, half_rows, jax.ShapeDtypeStr...  41.4 us
    pallas_call x1, Pallas kernels, body(): pl.pallas_call(finish, out_shape=(jax.ShapeDtypeStruct((NX * NS, PIECE, D...  1.35 us

profile of v9, /device:TPU:33, one launch (start us, length us, event | category | flops | bytes accessed | tf_op | source)
XLA Modules:
  0.0 44.7 jit_solution(10826698338134367392)
XLA Ops:
  1.9 41.4 %shard_map.95 = (bf16[16,8,1152]{2,1,0:T(8,128)(2,1)S(1)}, bf16[16,8,1152]{2,1,0:T(8,128)(2,1)S(1)}, f32[32,1,128]{2,1,0:T(1,128)S(1)}) custom-call(bf16[32,8,1152]{2,1,0:T(8,128)(2,1)} %bitcast.6, s32[1]{0:T(128)S(6)} %copy.10.time_hbm, f32[1]{0:T(128)S(6)} %copy.11.size_hbm, bf16[32,6912]{1,0:T(8,128)(2,1)} %mod_hbm.1, bf16[1728,1152]{1,0:T(8,128)(2,1)} %bitcast.4, ...), custom_call_target="tpu_custom_call" | custom-call | flops 2800000000 | bytes 12000000 | tf_op jit(solution)/shard_map/pallas_call | solution.py:495
  43.4 1.4 %shard_map.96 = (bf16[32,8,1152]{2,1,0:T(8,128)(2,1)}, f32[1]{0:T(128)}) custom-call(bf16[16,8,1152]{2,1,0:T(8,128)(2,1)S(1)} %get-tuple-element.7.first_ref, bf16[16,8,1152]{2,1,0:T(8,128)(2,1)S(1)} %get-tuple-element.8.second_ref, f32[32,1,128]{2,1,0:T(1,128)S(1)} %get-tuple-element.9.parts_ref), custom_call_target="tpu_custom_call" | custom-call | tf_op jit(solution)/shard_map/pallas_call | solution.py:523
